TPU v7x, 256 devices: a whole 4x4x8 slice. The times are simulated.
256 devices in a mesh: gy: 32 (over x, y, core), gz: 8 (over z).
Axes of the slice: x: 4, y: 4, z: 8, core: 2. Of those that a mesh axis runs over, the one named last changes fastest.
Arguments:
- field: float32 [10, 512, 32, 4096], P(None, 'gz', None, 'gy'), may hold values from -6 to 6
- tf_density: float32 [8], replicated, may hold values from 0.1 to 3
- tf_color: float32 [3, 8], replicated, may hold values from 0.1 to 1
Outputs:
- image: float32 [10, 4, 32, 4096], P(None, None, 'gz', 'gy')
All inputs are finite; a program needn't handle non-finite values.
Results may differ from a plain program's by a relative error of at most 0.000058.
Values sent between devices are 32-bit elements; how exact they have to be, the bound alone decides.
No kernel may reach another device: no remote copies, remote signals or barrier semaphores. Data moves between devices by JAX's collectives and lax.ppermute only.
A program may use at most 128 MiB of HBM per device.

v0:
```python
import jax
import jax.numpy as jnp
from jax import lax
from jax.sharding import PartitionSpec as P


def with_halo(cells, sides, width):
    for axis, dim in sides:
        count = lax.axis_size(axis)
        ends = count - 1
        head = lax.slice_in_dim(cells, 0, width, axis=dim)
        tail = lax.slice_in_dim(cells, cells.shape[dim] - width, cells.shape[dim], axis=dim)
        cells = jnp.concatenate(
            [
                lax.ppermute(tail, axis, [(i, (i + 1) % count) for i in range(ends)]),
                cells,
                lax.ppermute(head, axis, [((i + 1) % count, i) for i in range(ends)]),
            ],
            axis=dim,
        )
    return cells


def swapped(value, axis, distance):
    mask = 2**distance
    pairs = [(source, source ^ mask) for source in range(lax.axis_size(axis))]
    return lax.ppermute(value, axis, pairs)


def local_image(padded, tf_density, tf_color, lower, step):
    inner = padded[1:-1, :, 1:-1]
    widened = jnp.pad(padded, ((0, 0), (1, 1), (0, 0)))
    grad_z = 0.5 * (padded[2:, :, 1:-1] - padded[:-2, :, 1:-1])
    grad_x = 0.5 * (widened[1:-1, 2:, 1:-1] - widened[1:-1, :-2, 1:-1])
    grad_y = 0.5 * (padded[1:-1, :, 2:] - padded[1:-1, :, :-2])
    lit = 0.3 + 0.7 * jnp.abs(0.6 * grad_z + 0.48 * grad_x + 0.64 * grad_y) / jnp.sqrt(
        grad_z * grad_z + grad_x * grad_x + grad_y * grad_y + 1.0
    )
    count = tf_density.shape[0]
    tau = jnp.zeros(inner.shape, jnp.float32)
    tints = [jnp.zeros(inner.shape, jnp.float32) for channel in range(3)]
    for index in range(count):
        center = -2.0 + 4.0 * index / (count - 1)
        bump = jnp.exp(-2.0 * (inner - center) ** 2)
        tau = tau + tf_density[index] * bump
        tints = [tints[c] + tf_color[c, index] * bump for c in range(3)]
    tau = step * tau
    depth = tau.shape[0]
    ahead = jnp.dot(lower, tau.reshape(depth, -1), precision=lax.Precision.HIGHEST).reshape(
        tau.shape
    )
    weight = jnp.exp(-ahead) * (1.0 - jnp.exp(-tau)) * lit
    colors = [jnp.sum(weight * tints[c], axis=0) for c in range(3)]
    total = jnp.sum(tau, axis=0)
    return jnp.stack(colors + [total], axis=0)


def blend_over(front, back):
    return front + (1.0 - front[:, 3:4]) * back


def local(field, tf_density, tf_color):
    frames, depth, columns, rows = field.shape
    groups = lax.axis_size("gz")
    step = 1.5 / (depth * groups)
    padded = with_halo(field, (("gy", 3), ("gz", 1)), 1)
    counter = jnp.arange(depth)
    lower = (counter[:, None] > counter[None, :]).astype(jnp.float32)
    partial_value = lax.map(
        lambda slab: local_image(slab, tf_density, tf_color, lower, step), padded
    )
    piece = columns // groups
    opaque = jnp.concatenate([partial_value[:, :3], 1.0 - jnp.exp(-partial_value[:, 3:4])], axis=1)
    sliced = opaque.reshape(frames, 4, groups, piece, rows)
    place = lax.axis_index("gz")
    current = sliced
    for bit in range(groups.bit_length() - 1):
        number = current.shape[2]
        paired = current.reshape(frames, 4, number // 2, 2, piece, rows)
        mine = place // 2**bit % 2
        kept = lax.dynamic_index_in_dim(paired, mine, 3, keepdims=False)
        outgoing = lax.dynamic_index_in_dim(paired, 1 - mine, 3, keepdims=False)
        arrived = swapped(outgoing, "gz", bit)
        front = jnp.where(mine == 0, kept, arrived)
        back = jnp.where(mine == 0, arrived, kept)
        current = blend_over(front, back)
    return current.reshape(frames, 4, piece, rows)


def solution(mesh):
    placed = (P(None, "gz", None, "gy"), P(), P())
    return jax.shard_map(
        local, mesh=mesh, in_specs=placed, out_specs=P(None, None, "gz", "gy"), check_vma=False
    )
```

profile of v0, /device:TPU:28, one launch (start us, length us, event | category | flops | bytes accessed | tf_op | source)
XLA Modules:
  0.0 456.9 jit_solution(17916100971436631168)
XLA Ops:
  0.0 16.1 %fusion.22 = (f32[10,64,32,1]{3,2,1,0:T(8,128)}, f32[10,64,32,1]{3,2,1,0:T(8,128)}) fusion(f32[10,64,32,128]{3,2,1,0:T(8,128)} %param.5), kind=kLoop, calls=%fused_computation.59 | loop fusion | bytes 327680 | tf_op jit(solution)/shard_map/slice | solution.py:12
  16.1 6.6 %copy.8 = f32[10,64,32,1]{1,2,3,0:T(8,128)S(1)} copy(f32[10,64,32,1]{3,2,1,0:T(8,128)} %get-tuple-element.156) | data formatting | bytes 163840
  22.8 1.9 collective-permute-start
  24.7 6.7 %copy.9 = f32[10,64,32,1]{1,2,3,0:T(8,128)S(1)} copy(f32[10,64,32,1]{3,2,1,0:T(8,128)} %get-tuple-element.157) | data formatting | bytes 163840
  31.4 3.6 collective-permute-start.1
  35.0 6.3 %copy.6 = f32[10,64,32,1]{3,2,1,0:T(8,128)} copy(f32[10,64,32,1]{1,2,3,0:T(8,128)S(1)} %collective-permute-done) | data formatting | bytes 163840 | tf_op jit(solution)/shard_map/ppermute | solution.py:15
  41.3 6.2 %copy.7 = f32[10,64,32,1]{3,2,1,0:T(8,128)} copy(f32[10,64,32,1]{1,2,3,0:T(8,128)S(1)} %collective-permute-done.1) | data formatting | bytes 163840 | tf_op jit(solution)/shard_map/ppermute | solution.py:17
  49.2 3.8 collective-permute-start.2
  54.5 5.3 %collective-permute-done.2 = f32[10,1,32,130]{3,2,1,0:T(8,128)S(1)} collective-permute-done((f32[10,1,32,130]{3,2,1,0:T(8,128)S(1)}, f32[10,1,32,130]{3,2,1,0:T(8,128)S(1)}, u32[]{:S(2)}, u32[]{:S(2)}) %collective-permute-start.2) | collective-permute-done | bytes 166432 | tf_op jit(solution)/shard_map/ppermute | solution.py:15
  59.8 4.3 collective-permute-done.3
  64.1 22.6 %pad_maximum_fusion = f32[10,66,32,130]{3,2,1,0:T(8,128)} fusion(f32[10,1,32,130]{3,2,1,0:T(8,128)S(1)} %collective-permute-done.3, f32[10,64,32,1]{3,2,1,0:T(8,128)} %copy.7, f32[10,64,32,128]{3,2,1,0:T(8,128)} %param.5, f32[10,64,32,1]{3,2,1,0:T(8,128)} %copy.6, f32[10,1,32,130]{3,2,1,0:T(8,128)S(1)} %collective-permute-done.2), kind=kLoop, calls=%fused_computation.30 | loop fusion | flops 10982400 | bytes 21964800 | tf_op jit(solution)/shard_map/concatenate | solution.py:13
  86.7 340.2 %while.13 = (s32[]{:T(128)}, f32[10,4,32,128]{3,2,1,0:T(8,128)S(1)}, f32[8]{0:T(128)S(1)}, f32[10,66,32,130]{3,2,1,0:T(8,128)}, f32[3,8]{1,0:T(4,128)S(1)}, /*index=5*/s32[]{:T(128)}) while((s32[]{:T(128)}, f32[10,4,32,128]{3,2,1,0:T(8,128)S(1)}, f32[8]{0:T(128)S(1)}, f32[10,66,32,130]{3,2,1,0:T(8,128)}, f32[3,8]{1,0:T(4,128)S(1)}, ...), condition=%wide.region_5.6_spmd.clone, body=%wide.region_0.5_spmd.clone.sunk | while | flops 244883456 | bytes 21333452 | solution.py:69
  89.3 6.9 %fusion.34 = (f32[32,128]{1,0:T(8,128)S(1)}, f32[64,32,128]{2,1,0:T(8,128)S(1)}) fusion(f32[]{:T(128)} %bitcast.131, f32[]{:T(128)} %bitcast.132, f32[]{:T(128)} %bitcast.133, f32[]{:T(128)} %bitcast.134, f32[]{:T(128)} %bitcast.135, f32[]{:T(128)} %bitcast.136, f32[]{:T(128)} %bitcast.137, f32[66,32,130]{2,1,0:T(8,128)S(1)} %dynamic-slice_bitcast_fusion.4, ...), kind=kLoop, calls=%fused_computation.55.clone.1 | loop fusion | flops 10743808 | bytes 2113568 | tf_op jit(solution)/shard_map/while/body/eval_jaxpr/reduce_sum | solution.py:54
  98.8 8.7 %multiply_reduce_fusion.5 = (f32[32,128]{1,0:T(8,128)S(1)}, f32[64,32,128]{2,1,0:T(8,128)S(1)}) fusion(f32[]{:T(128)} %bitcast.140, f32[]{:T(128)} %bitcast.141, f32[]{:T(128)} %bitcast.142, f32[]{:T(128)} %bitcast.143, f32[]{:T(128)} %bitcast.144, f32[]{:T(128)} %bitcast.145, f32[]{:T(128)} %bitcast.146, f32[]{:T(128)} %bitcast.147, ...), kind=kLoop, calls=%fused_computation.15.clone.1 | loop fusion | flops 17297408 | bytes 10567712 | tf_op jit(solution)/shard_map/while/body/eval_jaxpr/reduce_sum | solution.py:53
  108.2 12.6 %multiply_reduce_fusion.6 = (f32[32,128]{1,0:T(8,128)S(1)}, f32[32,128]{1,0:T(8,128)S(1)}) fusion(f32[64,32,128]{2,1,0:T(8,128)S(1)} %get-tuple-element.245, f32[]{:T(128)} %bitcast.149, f32[]{:T(128)} %bitcast.150, f32[]{:T(128)} %bitcast.151, f32[]{:T(128)} %bitcast.152, f32[]{:T(128)} %bitcast.153, f32[]{:T(128)} %bitcast.154, f32[]{:T(128)} %bitcast.155, ...), kind=kLoop, calls=%fused_computation.16.clone.1 | loop fusion | flops 15196160 | bytes 2129984 | tf_op jit(solution)/shard_map/while/body/eval_jaxpr/reduce_sum | solution.py:53
  123.3 6.9 %fusion.34 = (f32[32,128]{1,0:T(8,128)S(1)}, f32[64,32,128]{2,1,0:T(8,128)S(1)}) fusion(f32[]{:T(128)} %bitcast.131, f32[]{:T(128)} %bitcast.132, f32[]{:T(128)} %bitcast.133, f32[]{:T(128)} %bitcast.134, f32[]{:T(128)} %bitcast.135, f32[]{:T(128)} %bitcast.136, f32[]{:T(128)} %bitcast.137, f32[66,32,130]{2,1,0:T(8,128)S(1)} %dynamic-slice_bitcast_fusion.4, ...), kind=kLoop, calls=%fused_computation.55.clone.1 | loop fusion | flops 10743808 | bytes 2113568 | tf_op jit(solution)/shard_map/while/body/eval_jaxpr/reduce_sum | solution.py:54
  132.8 8.7 %multiply_reduce_fusion.5 = (f32[32,128]{1,0:T(8,128)S(1)}, f32[64,32,128]{2,1,0:T(8,128)S(1)}) fusion(f32[]{:T(128)} %bitcast.140, f32[]{:T(128)} %bitcast.141, f32[]{:T(128)} %bitcast.142, f32[]{:T(128)} %bitcast.143, f32[]{:T(128)} %bitcast.144, f32[]{:T(128)} %bitcast.145, f32[]{:T(128)} %bitcast.146, f32[]{:T(128)} %bitcast.147, ...), kind=kLoop, calls=%fused_computation.15.clone.1 | loop fusion | flops 17297408 | bytes 10567712 | tf_op jit(solution)/shard_map/while/body/eval_jaxpr/reduce_sum | solution.py:53
  142.2 12.6 %multiply_reduce_fusion.6 = (f32[32,128]{1,0:T(8,128)S(1)}, f32[32,128]{1,0:T(8,128)S(1)}) fusion(f32[64,32,128]{2,1,0:T(8,128)S(1)} %get-tuple-element.245, f32[]{:T(128)} %bitcast.149, f32[]{:T(128)} %bitcast.150, f32[]{:T(128)} %bitcast.151, f32[]{:T(128)} %bitcast.152, f32[]{:T(128)} %bitcast.153, f32[]{:T(128)} %bitcast.154, f32[]{:T(128)} %bitcast.155, ...), kind=kLoop, calls=%fused_computation.16.clone.1 | loop fusion | flops 15196160 | bytes 2129984 | tf_op jit(solution)/shard_map/while/body/eval_jaxpr/reduce_sum | solution.py:53
  157.3 6.9 %fusion.34 = (f32[32,128]{1,0:T(8,128)S(1)}, f32[64,32,128]{2,1,0:T(8,128)S(1)}) fusion(f32[]{:T(128)} %bitcast.131, f32[]{:T(128)} %bitcast.132, f32[]{:T(128)} %bitcast.133, f32[]{:T(128)} %bitcast.134, f32[]{:T(128)} %bitcast.135, f32[]{:T(128)} %bitcast.136, f32[]{:T(128)} %bitcast.137, f32[66,32,130]{2,1,0:T(8,128)S(1)} %dynamic-slice_bitcast_fusion.4, ...), kind=kLoop, calls=%fused_computation.55.clone.1 | loop fusion | flops 10743808 | bytes 2113568 | tf_op jit(solution)/shard_map/while/body/eval_jaxpr/reduce_sum | solution.py:54
  166.8 8.7 %multiply_reduce_fusion.5 = (f32[32,128]{1,0:T(8,128)S(1)}, f32[64,32,128]{2,1,0:T(8,128)S(1)}) fusion(f32[]{:T(128)} %bitcast.140, f32[]{:T(128)} %bitcast.141, f32[]{:T(128)} %bitcast.142, f32[]{:T(128)} %bitcast.143, f32[]{:T(128)} %bitcast.144, f32[]{:T(128)} %bitcast.145, f32[]{:T(128)} %bitcast.146, f32[]{:T(128)} %bitcast.147, ...), kind=kLoop, calls=%fused_computation.15.clone.1 | loop fusion | flops 17297408 | bytes 10567712 | tf_op jit(solution)/shard_map/while/body/eval_jaxpr/reduce_sum | solution.py:53
  176.2 12.6 %multiply_reduce_fusion.6 = (f32[32,128]{1,0:T(8,128)S(1)}, f32[32,128]{1,0:T(8,128)S(1)}) fusion(f32[64,32,128]{2,1,0:T(8,128)S(1)} %get-tuple-element.245, f32[]{:T(128)} %bitcast.149, f32[]{:T(128)} %bitcast.150, f32[]{:T(128)} %bitcast.151, f32[]{:T(128)} %bitcast.152, f32[]{:T(128)} %bitcast.153, f32[]{:T(128)} %bitcast.154, f32[]{:T(128)} %bitcast.155, ...), kind=kLoop, calls=%fused_computation.16.clone.1 | loop fusion | flops 15196160 | bytes 2129984 | tf_op jit(solution)/shard_map/while/body/eval_jaxpr/reduce_sum | solution.py:53
  191.4 6.9 %fusion.34 = (f32[32,128]{1,0:T(8,128)S(1)}, f32[64,32,128]{2,1,0:T(8,128)S(1)}) fusion(f32[]{:T(128)} %bitcast.131, f32[]{:T(128)} %bitcast.132, f32[]{:T(128)} %bitcast.133, f32[]{:T(128)} %bitcast.134, f32[]{:T(128)} %bitcast.135, f32[]{:T(128)} %bitcast.136, f32[]{:T(128)} %bitcast.137, f32[66,32,130]{2,1,0:T(8,128)S(1)} %dynamic-slice_bitcast_fusion.4, ...), kind=kLoop, calls=%fused_computation.55.clone.1 | loop fusion | flops 10743808 | bytes 2113568 | tf_op jit(solution)/shard_map/while/body/eval_jaxpr/reduce_sum | solution.py:54
  200.9 8.7 %multiply_reduce_fusion.5 = (f32[32,128]{1,0:T(8,128)S(1)}, f32[64,32,128]{2,1,0:T(8,128)S(1)}) fusion(f32[]{:T(128)} %bitcast.140, f32[]{:T(128)} %bitcast.141, f32[]{:T(128)} %bitcast.142, f32[]{:T(128)} %bitcast.143, f32[]{:T(128)} %bitcast.144, f32[]{:T(128)} %bitcast.145, f32[]{:T(128)} %bitcast.146, f32[]{:T(128)} %bitcast.147, ...), kind=kLoop, calls=%fused_computation.15.clone.1 | loop fusion | flops 17297408 | bytes 10567712 | tf_op jit(solution)/shard_map/while/body/eval_jaxpr/reduce_sum | solution.py:53
  210.2 12.6 %multiply_reduce_fusion.6 = (f32[32,128]{1,0:T(8,128)S(1)}, f32[32,128]{1,0:T(8,128)S(1)}) fusion(f32[64,32,128]{2,1,0:T(8,128)S(1)} %get-tuple-element.245, f32[]{:T(128)} %bitcast.149, f32[]{:T(128)} %bitcast.150, f32[]{:T(128)} %bitcast.151, f32[]{:T(128)} %bitcast.152, f32[]{:T(128)} %bitcast.153, f32[]{:T(128)} %bitcast.154, f32[]{:T(128)} %bitcast.155, ...), kind=kLoop, calls=%fused_computation.16.clone.1 | loop fusion | flops 15196160 | bytes 2129984 | tf_op jit(solution)/shard_map/while/body/eval_jaxpr/reduce_sum | solution.py:53
  225.4 6.9 %fusion.34 = (f32[32,128]{1,0:T(8,128)S(1)}, f32[64,32,128]{2,1,0:T(8,128)S(1)}) fusion(f32[]{:T(128)} %bitcast.131, f32[]{:T(128)} %bitcast.132, f32[]{:T(128)} %bitcast.133, f32[]{:T(128)} %bitcast.134, f32[]{:T(128)} %bitcast.135, f32[]{:T(128)} %bitcast.136, f32[]{:T(128)} %bitcast.137, f32[66,32,130]{2,1,0:T(8,128)S(1)} %dynamic-slice_bitcast_fusion.4, ...), kind=kLoop, calls=%fused_computation.55.clone.1 | loop fusion | flops 10743808 | bytes 2113568 | tf_op jit(solution)/shard_map/while/body/eval_jaxpr/reduce_sum | solution.py:54
  234.9 8.7 %multiply_reduce_fusion.5 = (f32[32,128]{1,0:T(8,128)S(1)}, f32[64,32,128]{2,1,0:T(8,128)S(1)}) fusion(f32[]{:T(128)} %bitcast.140, f32[]{:T(128)} %bitcast.141, f32[]{:T(128)} %bitcast.142, f32[]{:T(128)} %bitcast.143, f32[]{:T(128)} %bitcast.144, f32[]{:T(128)} %bitcast.145, f32[]{:T(128)} %bitcast.146, f32[]{:T(128)} %bitcast.147, ...), kind=kLoop, calls=%fused_computation.15.clone.1 | loop fusion | flops 17297408 | bytes 10567712 | tf_op jit(solution)/shard_map/while/body/eval_jaxpr/reduce_sum | solution.py:53
  244.3 12.6 %multiply_reduce_fusion.6 = (f32[32,128]{1,0:T(8,128)S(1)}, f32[32,128]{1,0:T(8,128)S(1)}) fusion(f32[64,32,128]{2,1,0:T(8,128)S(1)} %get-tuple-element.245, f32[]{:T(128)} %bitcast.149, f32[]{:T(128)} %bitcast.150, f32[]{:T(128)} %bitcast.151, f32[]{:T(128)} %bitcast.152, f32[]{:T(128)} %bitcast.153, f32[]{:T(128)} %bitcast.154, f32[]{:T(128)} %bitcast.155, ...), kind=kLoop, calls=%fused_computation.16.clone.1 | loop fusion | flops 15196160 | bytes 2129984 | tf_op jit(solution)/shard_map/while/body/eval_jaxpr/reduce_sum | solution.py:53
  259.4 6.9 %fusion.34 = (f32[32,128]{1,0:T(8,128)S(1)}, f32[64,32,128]{2,1,0:T(8,128)S(1)}) fusion(f32[]{:T(128)} %bitcast.131, f32[]{:T(128)} %bitcast.132, f32[]{:T(128)} %bitcast.133, f32[]{:T(128)} %bitcast.134, f32[]{:T(128)} %bitcast.135, f32[]{:T(128)} %bitcast.136, f32[]{:T(128)} %bitcast.137, f32[66,32,130]{2,1,0:T(8,128)S(1)} %dynamic-slice_bitcast_fusion.4, ...), kind=kLoop, calls=%fused_computation.55.clone.1 | loop fusion | flops 10743808 | bytes 2113568 | tf_op jit(solution)/shard_map/while/body/eval_jaxpr/reduce_sum | solution.py:54
  268.9 8.7 %multiply_reduce_fusion.5 = (f32[32,128]{1,0:T(8,128)S(1)}, f32[64,32,128]{2,1,0:T(8,128)S(1)}) fusion(f32[]{:T(128)} %bitcast.140, f32[]{:T(128)} %bitcast.141, f32[]{:T(128)} %bitcast.142, f32[]{:T(128)} %bitcast.143, f32[]{:T(128)} %bitcast.144, f32[]{:T(128)} %bitcast.145, f32[]{:T(128)} %bitcast.146, f32[]{:T(128)} %bitcast.147, ...), kind=kLoop, calls=%fused_computation.15.clone.1 | loop fusion | flops 17297408 | bytes 10567712 | tf_op jit(solution)/shard_map/while/body/eval_jaxpr/reduce_sum | solution.py:53
  278.3 12.6 %multiply_reduce_fusion.6 = (f32[32,128]{1,0:T(8,128)S(1)}, f32[32,128]{1,0:T(8,128)S(1)}) fusion(f32[64,32,128]{2,1,0:T(8,128)S(1)} %get-tuple-element.245, f32[]{:T(128)} %bitcast.149, f32[]{:T(128)} %bitcast.150, f32[]{:T(128)} %bitcast.151, f32[]{:T(128)} %bitcast.152, f32[]{:T(128)} %bitcast.153, f32[]{:T(128)} %bitcast.154, f32[]{:T(128)} %bitcast.155, ...), kind=kLoop, calls=%fused_computation.16.clone.1 | loop fusion | flops 15196160 | bytes 2129984 | tf_op jit(solution)/shard_map/while/body/eval_jaxpr/reduce_sum | solution.py:53
  293.4 6.9 %fusion.34 = (f32[32,128]{1,0:T(8,128)S(1)}, f32[64,32,128]{2,1,0:T(8,128)S(1)}) fusion(f32[]{:T(128)} %bitcast.131, f32[]{:T(128)} %bitcast.132, f32[]{:T(128)} %bitcast.133, f32[]{:T(128)} %bitcast.134, f32[]{:T(128)} %bitcast.135, f32[]{:T(128)} %bitcast.136, f32[]{:T(128)} %bitcast.137, f32[66,32,130]{2,1,0:T(8,128)S(1)} %dynamic-slice_bitcast_fusion.4, ...), kind=kLoop, calls=%fused_computation.55.clone.1 | loop fusion | flops 10743808 | bytes 2113568 | tf_op jit(solution)/shard_map/while/body/eval_jaxpr/reduce_sum | solution.py:54
  302.9 8.7 %multiply_reduce_fusion.5 = (f32[32,128]{1,0:T(8,128)S(1)}, f32[64,32,128]{2,1,0:T(8,128)S(1)}) fusion(f32[]{:T(128)} %bitcast.140, f32[]{:T(128)} %bitcast.141, f32[]{:T(128)} %bitcast.142, f32[]{:T(128)} %bitcast.143, f32[]{:T(128)} %bitcast.144, f32[]{:T(128)} %bitcast.145, f32[]{:T(128)} %bitcast.146, f32[]{:T(128)} %bitcast.147, ...), kind=kLoop, calls=%fused_computation.15.clone.1 | loop fusion | flops 17297408 | bytes 10567712 | tf_op jit(solution)/shard_map/while/body/eval_jaxpr/reduce_sum | solution.py:53
  312.3 12.6 %multiply_reduce_fusion.6 = (f32[32,128]{1,0:T(8,128)S(1)}, f32[32,128]{1,0:T(8,128)S(1)}) fusion(f32[64,32,128]{2,1,0:T(8,128)S(1)} %get-tuple-element.245, f32[]{:T(128)} %bitcast.149, f32[]{:T(128)} %bitcast.150, f32[]{:T(128)} %bitcast.151, f32[]{:T(128)} %bitcast.152, f32[]{:T(128)} %bitcast.153, f32[]{:T(128)} %bitcast.154, f32[]{:T(128)} %bitcast.155, ...), kind=kLoop, calls=%fused_computation.16.clone.1 | loop fusion | flops 15196160 | bytes 2129984 | tf_op jit(solution)/shard_map/while/body/eval_jaxpr/reduce_sum | solution.py:53
  327.4 6.9 %fusion.34 = (f32[32,128]{1,0:T(8,128)S(1)}, f32[64,32,128]{2,1,0:T(8,128)S(1)}) fusion(f32[]{:T(128)} %bitcast.131, f32[]{:T(128)} %bitcast.132, f32[]{:T(128)} %bitcast.133, f32[]{:T(128)} %bitcast.134, f32[]{:T(128)} %bitcast.135, f32[]{:T(128)} %bitcast.136, f32[]{:T(128)} %bitcast.137, f32[66,32,130]{2,1,0:T(8,128)S(1)} %dynamic-slice_bitcast_fusion.4, ...), kind=kLoop, calls=%fused_computation.55.clone.1 | loop fusion | flops 10743808 | bytes 2113568 | tf_op jit(solution)/shard_map/while/body/eval_jaxpr/reduce_sum | solution.py:54
  336.9 8.7 %multiply_reduce_fusion.5 = (f32[32,128]{1,0:T(8,128)S(1)}, f32[64,32,128]{2,1,0:T(8,128)S(1)}) fusion(f32[]{:T(128)} %bitcast.140, f32[]{:T(128)} %bitcast.141, f32[]{:T(128)} %bitcast.142, f32[]{:T(128)} %bitcast.143, f32[]{:T(128)} %bitcast.144, f32[]{:T(128)} %bitcast.145, f32[]{:T(128)} %bitcast.146, f32[]{:T(128)} %bitcast.147, ...), kind=kLoop, calls=%fused_computation.15.clone.1 | loop fusion | flops 17297408 | bytes 10567712 | tf_op jit(solution)/shard_map/while/body/eval_jaxpr/reduce_sum | solution.py:53
  346.3 12.6 %multiply_reduce_fusion.6 = (f32[32,128]{1,0:T(8,128)S(1)}, f32[32,128]{1,0:T(8,128)S(1)}) fusion(f32[64,32,128]{2,1,0:T(8,128)S(1)} %get-tuple-element.245, f32[]{:T(128)} %bitcast.149, f32[]{:T(128)} %bitcast.150, f32[]{:T(128)} %bitcast.151, f32[]{:T(128)} %bitcast.152, f32[]{:T(128)} %bitcast.153, f32[]{:T(128)} %bitcast.154, f32[]{:T(128)} %bitcast.155, ...), kind=kLoop, calls=%fused_computation.16.clone.1 | loop fusion | flops 15196160 | bytes 2129984 | tf_op jit(solution)/shard_map/while/body/eval_jaxpr/reduce_sum | solution.py:53
  361.5 6.9 %fusion.34 = (f32[32,128]{1,0:T(8,128)S(1)}, f32[64,32,128]{2,1,0:T(8,128)S(1)}) fusion(f32[]{:T(128)} %bitcast.131, f32[]{:T(128)} %bitcast.132, f32[]{:T(128)} %bitcast.133, f32[]{:T(128)} %bitcast.134, f32[]{:T(128)} %bitcast.135, f32[]{:T(128)} %bitcast.136, f32[]{:T(128)} %bitcast.137, f32[66,32,130]{2,1,0:T(8,128)S(1)} %dynamic-slice_bitcast_fusion.4, ...), kind=kLoop, calls=%fused_computation.55.clone.1 | loop fusion | flops 10743808 | bytes 2113568 | tf_op jit(solution)/shard_map/while/body/eval_jaxpr/reduce_sum | solution.py:54
  371.0 8.7 %multiply_reduce_fusion.5 = (f32[32,128]{1,0:T(8,128)S(1)}, f32[64,32,128]{2,1,0:T(8,128)S(1)}) fusion(f32[]{:T(128)} %bitcast.140, f32[]{:T(128)} %bitcast.141, f32[]{:T(128)} %bitcast.142, f32[]{:T(128)} %bitcast.143, f32[]{:T(128)} %bitcast.144, f32[]{:T(128)} %bitcast.145, f32[]{:T(128)} %bitcast.146, f32[]{:T(128)} %bitcast.147, ...), kind=kLoop, calls=%fused_computation.15.clone.1 | loop fusion | flops 17297408 | bytes 10567712 | tf_op jit(solution)/shard_map/while/body/eval_jaxpr/reduce_sum | solution.py:53
  380.3 12.6 %multiply_reduce_fusion.6 = (f32[32,128]{1,0:T(8,128)S(1)}, f32[32,128]{1,0:T(8,128)S(1)}) fusion(f32[64,32,128]{2,1,0:T(8,128)S(1)} %get-tuple-element.245, f32[]{:T(128)} %bitcast.149, f32[]{:T(128)} %bitcast.150, f32[]{:T(128)} %bitcast.151, f32[]{:T(128)} %bitcast.152, f32[]{:T(128)} %bitcast.153, f32[]{:T(128)} %bitcast.154, f32[]{:T(128)} %bitcast.155, ...), kind=kLoop, calls=%fused_computation.16.clone.1 | loop fusion | flops 15196160 | bytes 2129984 | tf_op jit(solution)/shard_map/while/body/eval_jaxpr/reduce_sum | solution.py:53
  395.5 6.9 %fusion.34 = (f32[32,128]{1,0:T(8,128)S(1)}, f32[64,32,128]{2,1,0:T(8,128)S(1)}) fusion(f32[]{:T(128)} %bitcast.131, f32[]{:T(128)} %bitcast.132, f32[]{:T(128)} %bitcast.133, f32[]{:T(128)} %bitcast.134, f32[]{:T(128)} %bitcast.135, f32[]{:T(128)} %bitcast.136, f32[]{:T(128)} %bitcast.137, f32[66,32,130]{2,1,0:T(8,128)S(1)} %dynamic-slice_bitcast_fusion.4, ...), kind=kLoop, calls=%fused_computation.55.clone.1 | loop fusion | flops 10743808 | bytes 2113568 | tf_op jit(solution)/shard_map/while/body/eval_jaxpr/reduce_sum | solution.py:54
  405.0 8.7 %multiply_reduce_fusion.5 = (f32[32,128]{1,0:T(8,128)S(1)}, f32[64,32,128]{2,1,0:T(8,128)S(1)}) fusion(f32[]{:T(128)} %bitcast.140, f32[]{:T(128)} %bitcast.141, f32[]{:T(128)} %bitcast.142, f32[]{:T(128)} %bitcast.143, f32[]{:T(128)} %bitcast.144, f32[]{:T(128)} %bitcast.145, f32[]{:T(128)} %bitcast.146, f32[]{:T(128)} %bitcast.147, ...), kind=kLoop, calls=%fused_computation.15.clone.1 | loop fusion | flops 17297408 | bytes 10567712 | tf_op jit(solution)/shard_map/while/body/eval_jaxpr/reduce_sum | solution.py:53
  414.4 12.6 %multiply_reduce_fusion.6 = (f32[32,128]{1,0:T(8,128)S(1)}, f32[32,128]{1,0:T(8,128)S(1)}) fusion(f32[64,32,128]{2,1,0:T(8,128)S(1)} %get-tuple-element.245, f32[]{:T(128)} %bitcast.149, f32[]{:T(128)} %bitcast.150, f32[]{:T(128)} %bitcast.151, f32[]{:T(128)} %bitcast.152, f32[]{:T(128)} %bitcast.153, f32[]{:T(128)} %bitcast.154, f32[]{:T(128)} %bitcast.155, ...), kind=kLoop, calls=%fused_computation.16.clone.1 | loop fusion | flops 15196160 | bytes 2129984 | tf_op jit(solution)/shard_map/while/body/eval_jaxpr/reduce_sum | solution.py:53
  427.2 2.0 collective-permute-start.4
  429.2 6.5 %collective-permute-done.4 = f32[10,4,4,4,128]{4,3,2,1,0:T(4,128)S(1)} collective-permute-done((f32[10,4,4,4,128]{4,3,2,1,0:T(4,128)S(1)}, f32[10,4,4,4,128]{4,3,2,1,0:T(4,128)S(1)}, u32[]{:S(2)}, u32[]{:S(2)}) %collective-permute-start.4) | collective-permute-done | bytes 327712 | tf_op jit(solution)/shard_map/ppermute | solution.py:27
  436.0 5.4 %collective-permute-start.5 = (f32[10,4,2,4,128]{4,3,2,1,0:T(4,128)S(1)}, f32[10,4,2,4,128]{4,3,2,1,0:T(4,128)S(1)}, u32[]{:S(2)}, u32[]{:S(2)}) collective-permute-start(f32[10,4,2,4,128]{4,3,2,1,0:T(4,128)S(1)} %dynamic-slice_bitcast_fusion.2), channel_id=1, source_target_pairs={{0,2},{1,3},{2,0},{3,1},{4,6},{5,7},{6,4},{7,5},{8,10},{9,11},{10,... | collective-permute-start | bytes 491528 | tf_op jit(solution)/shard_map/ppermute | solution.py:27
  441.5 5.7 %collective-permute-done.5 = f32[10,4,2,4,128]{4,3,2,1,0:T(4,128)S(1)} collective-permute-done((f32[10,4,2,4,128]{4,3,2,1,0:T(4,128)S(1)}, f32[10,4,2,4,128]{4,3,2,1,0:T(4,128)S(1)}, u32[]{:S(2)}, u32[]{:S(2)}) %collective-permute-start.5) | collective-permute-done | bytes 163872 | tf_op jit(solution)/shard_map/ppermute | solution.py:27
  447.4 2.9 collective-permute-start.6
  450.2 6.0 %collective-permute-done.6 = f32[10,4,1,4,128]{4,3,2,1,0:T(4,128)S(1)} collective-permute-done((f32[10,4,1,4,128]{4,3,2,1,0:T(4,128)S(1)}, f32[10,4,1,4,128]{4,3,2,1,0:T(4,128)S(1)}, u32[]{:S(2)}, u32[]{:S(2)}) %collective-permute-start.6) | collective-permute-done | bytes 81952 | tf_op jit(solution)/shard_map/ppermute | solution.py:27
  (94 shorter events, 62.6 us)
Async XLA Ops:
  22.8 12.2 %collective-permute-start = (f32[10,64,32,1]{1,2,3,0:T(8,128)S(1)}, f32[10,64,32,1]{1,2,3,0:T(8,128)S(1)}, u32[]{:S(2)}, u32[]{:S(2)}) collective-permute-start(f32[10,64,32,1]{1,2,3,0:T(8,128)S(1)} %copy.8), channel_id=1, source_target_pairs={{0,8},{8,16},{16,24},{24,32},{32,40},{40,48},{48,56},{56,64},{64,7... | collective-permute-start | bytes 245768 | tf_op jit(solution)/shard_map/ppermute | solution.py:15
  31.4 10.0 %collective-permute-start.1 = (f32[10,64,32,1]{1,2,3,0:T(8,128)S(1)}, f32[10,64,32,1]{1,2,3,0:T(8,128)S(1)}, u32[]{:S(2)}, u32[]{:S(2)}) collective-permute-start(f32[10,64,32,1]{1,2,3,0:T(8,128)S(1)} %copy.9), channel_id=1, source_target_pairs={{8,0},{16,8},{24,16},{32,24},{40,32},{48,40},{56,48},{64,56},{72,6... | collective-permute-start | bytes 245768 | tf_op jit(solution)/shard_map/ppermute | solution.py:17
  49.2 10.7 %collective-permute-start.2 = (f32[10,1,32,130]{3,2,1,0:T(8,128)S(1)}, f32[10,1,32,130]{3,2,1,0:T(8,128)S(1)}, u32[]{:S(2)}, u32[]{:S(2)}) collective-permute-start(f32[10,1,32,130]{3,2,1,0:T(8,128)S(1)} %get-tuple-element.154), channel_id=1, source_target_pairs={{0,1},{1,2},{2,3},{3,4},{4,5},{5,6},{6,7},{8,9},{9,10},{10,11},{11... | collective-permute-start | bytes 499208 | tf_op jit(solution)/shard_map/ppermute | solution.py:15
  53.0 11.1 %collective-permute-start.3 = (f32[10,1,32,130]{3,2,1,0:T(8,128)S(1)}, f32[10,1,32,130]{3,2,1,0:T(8,128)S(1)}, u32[]{:S(2)}, u32[]{:S(2)}) collective-permute-start(f32[10,1,32,130]{3,2,1,0:T(8,128)S(1)} %get-tuple-element.155), channel_id=1, source_target_pairs={{1,0},{2,1},{3,2},{4,3},{5,4},{6,5},{7,6},{9,8},{10,9},{11,10},{12... | collective-permute-start | bytes 499208 | tf_op jit(solution)/shard_map/ppermute | solution.py:17
  54.5 32.2 %copy-start = (f32[3,8]{1,0:T(4,128)S(1)}, f32[3,8]{1,0:T(4,128)}, u32[]{:S(2)}) copy-start(f32[3,8]{1,0:T(4,128)} %param.7) | copy-start | bytes 292
  54.5 32.2 %copy-start.1 = (f32[8]{0:T(128)S(1)}, f32[8]{0:T(128)}, u32[]{:S(2)}) copy-start(f32[8]{0:T(128)} %param.6) | copy-start | bytes 100
  427.2 8.6 %collective-permute-start.4 = (f32[10,4,4,4,128]{4,3,2,1,0:T(4,128)S(1)}, f32[10,4,4,4,128]{4,3,2,1,0:T(4,128)S(1)}, u32[]{:S(2)}, u32[]{:S(2)}) collective-permute-start(f32[10,4,4,4,128]{4,3,2,1,0:T(4,128)S(1)} %dynamic-slice_bitcast_fusion.1), channel_id=1, source_target_pairs={{0,1},{1,0},{2,3},{3,2},{4,5},{5,4},{6,7},{7,6},{8,9},{9,8},{10,11... | collective-permute-start | bytes 983048 | tf_op jit(solution)/shard_map/ppermute | solution.py:27
  436.0 11.2 %collective-permute-start.5 = (f32[10,4,2,4,128]{4,3,2,1,0:T(4,128)S(1)}, f32[10,4,2,4,128]{4,3,2,1,0:T(4,128)S(1)}, u32[]{:S(2)}, u32[]{:S(2)}) collective-permute-start(f32[10,4,2,4,128]{4,3,2,1,0:T(4,128)S(1)} %dynamic-slice_bitcast_fusion.2), channel_id=1, source_target_pairs={{0,2},{1,3},{2,0},{3,1},{4,6},{5,7},{6,4},{7,5},{8,10},{9,11},{10,... | collective-permute-start | bytes 491528 | tf_op jit(solution)/shard_map/ppermute | solution.py:27
  447.4 8.9 %collective-permute-start.6 = (f32[10,4,1,4,128]{4,3,2,1,0:T(4,128)S(1)}, f32[10,4,1,4,128]{4,3,2,1,0:T(4,128)S(1)}, u32[]{:S(2)}, u32[]{:S(2)}) collective-permute-start(f32[10,4,1,4,128]{4,3,2,1,0:T(4,128)S(1)} %constant_dynamic-slice_fusion), channel_id=1, source_target_pairs={{0,4},{1,5},{2,6},{3,7},{4,0},{5,1},{6,2},{7,3},{8,12},{9,13},{10,... | collective-permute-start | bytes 245768 | tf_op jit(solution)/shard_map/ppermute | solution.py:27
where the time goes:
time: 464 us; the launch traced here: 457 us
  other arithmetic  307 us (66%)
  local copies, waits for them, and re-layouts  83.1 us (18%)
  waiting for transfers between devices  27.8 us (6%)
  starting transfers between devices  21.2 us (5%)
  matrix products  17.2 us (4%)
    reduce_sum x20, other arithmetic, local_image(): colors = [jnp.sum(weight * tints[c], axis=0) for c in range(3)]  213 us
    reduce_sum x10, other arithmetic, local_image(): total = jnp.sum(tau, axis=0)  68.5 us
    concatenate x1, other arithmetic, with_halo(): jnp.concatenate([lax.ppermute(tail, axis, [(i, (i + 1) % count) for i in...  22.6 us
    squeeze x10, local copies, waits for them, and re-layouts, local(): lax.map(lambda slab: local_image(slab, tf_density, tf_color, lower, step)...  18.5 us
    ppermute x3, waiting for transfers between devices, swapped(): return lax.ppermute(value, axis, pairs)  18.3 us
    dot_general x10, matrix products, local_image(): jnp.dot(lower, tau.reshape(depth, -1), precision=lax.Precision.HIGHEST)  17.2 us
    slice x1, local copies, waits for them, and re-layouts, with_halo(): lax.slice_in_dim(cells, cells.shape[dim] - width, cells.shape[dim], axis=...  16.1 us
    slice x20, local copies, waits for them, and re-layouts, local_image(): tints = [tints[c] + tf_color[c, index] * bump for c in range(3)]  13.7 us
  transfers between devices with their start and end apart: 7, of which 5 were waited for; matrix products, arithmetic and copies ran while one was open for 3% of the time, Pallas kernels for 0%

commit v1 on v0

v1 whole, which is shorter than its diff:
```python
import functools
import math

import jax
import jax.numpy as jnp
from jax import lax
from jax.experimental import pallas as pl
from jax.experimental.pallas import tpu as pltpu
from jax.sharding import PartitionSpec as P

BUMPS = 8
BASE = 3
SPACING = 4.0 / (BUMPS - 1)
CENTRE = -2.0 + SPACING * BASE
LOG2E = math.log2(math.e)
RATE = 4.0 * SPACING * LOG2E
BELL = -2.0 * LOG2E / (RATE * RATE)
FALL = [math.exp(-2.0 * ((j - BASE) * SPACING) ** 2) for j in range(BUMPS)]
LANES = 128
TILE = 8
PITCH = 40


def edges_kernel(odd_ref, field_ref, outer_ref, second_ref, pair_ref, next_ref, cells, sems):
    frames, depth, columns = field_ref.shape[:3]
    lane = lax.broadcasted_iota(jnp.int32, (TILE, LANES), 1)
    odd_z = odd_ref[1] == 1
    spans = [slice(t, t + TILE) for t in range(0, columns, TILE)]

    def load(f):
        return pltpu.make_async_copy(field_ref.at[f], cells.at[f], sems.at[f])

    for f in range(frames):
        load(f).start()

    def one_frame(f, _):
        load(f).wait()
        outer = [jnp.zeros((TILE, LANES), jnp.float32) for _ in spans]
        second = [jnp.zeros((TILE, LANES), jnp.float32) for _ in spans]
        for z in range(depth):
            own = (lane >> 1) == z
            near = (lane == (2 * z - 1) % LANES) | (lane == (2 * z + 2) % LANES)
            for t, span in enumerate(spans):
                turned = pltpu.roll(cells[f, z, span, :], (2 * z + 1) % LANES, 1)
                outer[t] = jnp.where(own, turned, outer[t])
                second[t] = jnp.where(near, turned, second[t])
        for t, span in enumerate(spans):
            outer_ref[f, span, :] = outer[t]
            second_ref[f, span, :] = second[t]
            front, back = cells[f, 0, span, :], cells[f, depth - 1, span, :]
            pair_ref[f, span, :] = jnp.where(odd_z, front, back)
            next_ref[f, span, :] = jnp.where(odd_z, back, front)
        return 0

    lax.fori_loop(0, frames, one_frame, 0)


def render_kernel(
    odd_ref,
    density_ref,
    color_ref,
    z1_ref,
    z2_ref,
    y1_ref,
    y2_ref,
    second_ref,
    field_ref,
    *rest,
    step,
    start,
):
    kept_ref, sent_ref, cells, sems = rest[-4:]
    frame, frames = pl.program_id(0), pl.num_programs(0)
    depth, columns = field_ref.shape[1], field_ref.shape[2]
    tiles = columns // TILE
    slot = lax.rem(frame, 2)

    def load(which, into):
        return pltpu.make_async_copy(
            field_ref.at[start + which], cells.at[into, pl.ds(1, depth), pl.ds(TILE, columns), :], sems.at[into]
        )

    @pl.when(frame == 0)
    def _():
        load(0, 0).start()
        for into in range(2):
            for plane in range(depth + 3):
                cells[into, plane, 0:TILE, :] = jnp.zeros((TILE, LANES), jnp.float32)

    @pl.when(frame + 1 < frames)
    def _():
        load(frame + 1, 1 - slot).start()

    odd_y, odd_z, late = odd_ref[0] == 1, odd_ref[1] == 1, odd_ref[2]
    lane = lax.broadcasted_iota(jnp.int32, (TILE, LANES), 1)
    even_lane = (lane & 1) == 0
    edge_lane = (lane == 0) | (lane == LANES - 1)

    rows = cells.reshape(2 * cells.shape[1] * PITCH, LANES)
    first = slot * (cells.shape[1] * PITCH) + TILE

    for t in range(tiles):
        here = slice(t * TILE, (t + 1) * TILE)
        a, b = z1_ref[0, here, :], z2_ref[0, here, :]
        cells[slot, 0, TILE + t * TILE : TILE + (t + 1) * TILE, :] = jnp.where(odd_z, a, b)
        cells[slot, depth + 1, TILE + t * TILE : TILE + (t + 1) * TILE, :] = jnp.where(odd_z, b, a)

    scale = [-LOG2E * step * FALL[j] for j in range(BUMPS)]
    dens = [jnp.full((TILE, LANES), density_ref[j] * scale[j], jnp.float32) for j in range(BUMPS)]
    load(frame, slot).wait()

    def one_tile(t, _):
        top = first + t * TILE
        here = pl.ds(pl.multiple_of(t * TILE, TILE), TILE)
        a, b = y1_ref[0, here, :], y2_ref[0, here, :]
        left, right = jnp.where(odd_y, a, b), jnp.where(odd_y, b, a)
        second = second_ref[0, here, :]
        rim = jnp.where(
            even_lane,
            pltpu.roll(right, LANES - 1, 1) - pltpu.roll(second, 1, 1),
            pltpu.roll(second, LANES - 1, 1) - pltpu.roll(left, 1, 1),
        )

        def one_depth(z, carry):
            total, clear, before, cell = carry[:4]
            sums = list(carry[4:])
            row = top + (z + 1) * PITCH
            after = rows[pl.ds(pl.multiple_of(row + PITCH, TILE), TILE), :]
            gz = after - before
            gx = rows[pl.ds(row + 1, TILE), :] - rows[pl.ds(row - 1, TILE), :]
            gy = pltpu.roll(cell, LANES - 1, 1) - pltpu.roll(cell, 1, 1)
            gy = jnp.where(edge_lane, pltpu.roll(rim, LANES - 1 - 2 * z, 1), gy)
            slope = jnp.abs(gz + 0.8 * gx + (16.0 / 15.0) * gy)
            lit = (0.3 / 0.42) + slope * lax.rsqrt(gz * gz + gx * gx + gy * gy + 4.0)
            q = cell * RATE - (CENTRE * RATE)
            up = jnp.exp2(q)
            down = jnp.exp2(-q)
            bell = jnp.exp2(q * q * BELL)
            high = (((dens[7] * up + dens[6]) * up + dens[5]) * up + dens[4]) * up + dens[3]
            low = ((dens[0] * down + dens[1]) * down + dens[2]) * down
            total = total + (high + low) * bell
            behind = jnp.exp2(total)
            power = (clear - behind) * lit * bell
            sums[BASE] = sums[BASE] + power
            rise = power
            for j in range(BASE + 1, BUMPS):
                rise = rise * up
                sums[j] = sums[j] + rise
            drop = power
            for j in range(BASE - 1, -1, -1):
                drop = drop * down
                sums[j] = sums[j] + drop
            return (total, behind, cell, after, *sums)

        zero = jnp.zeros((TILE, LANES), jnp.float32)
        begin = (
            zero,
            zero + 1.0,
            rows[pl.ds(pl.multiple_of(top, TILE), TILE), :],
            rows[pl.ds(pl.multiple_of(top + PITCH, TILE), TILE), :],
        ) + (zero,) * BUMPS
        final = begin
        for z in range(depth):
            final = one_depth(z, final)
        total, sums = final[0], final[4:]
        parts = []
        for c in range(3):
            parts.append(
                functools.reduce(
                    jnp.add, [(color_ref[c, j] * (0.42 * FALL[j])) * sums[j] for j in range(BUMPS)]
                )
            )
        parts.append(total)
        keep_first = late == jnp.where(t >= 2, 1, 0)
        share = jnp.where(t == 0, 0, jnp.where(t == 1, 2, jnp.where(t == 2, 3, 1)))
        for c in range(4):
            kept_ref[share, 0, c, :, :] = jnp.where(keep_first, parts[c][0:4], parts[c][4:8])
            sent_ref[share, 0, c, :, :] = jnp.where(keep_first, parts[c][4:8], parts[c][0:4])
        return 0

    lax.fori_loop(0, tiles, one_tile, 0)


def joined(kept, arrived, in_front):
    front, back = jnp.where(in_front, kept, arrived), jnp.where(in_front, arrived, kept)
    clear = jnp.exp2(front[:, :, 3:4])
    return jnp.concatenate([front[:, :, :3] + clear * back[:, :, :3], front[:, :, 3:] + back[:, :, 3:]], axis=2)


def halves(value, late):
    half = value.shape[0] // 2
    kept = jnp.where(late == 0, value[:half], value[half:])
    return kept, jnp.where(late == 0, value[half:], value[:half])


def pairs_of(count, offset):
    lows = range(offset, count - 1, 2)
    return [(i, i + 1) for i in lows] + [(i + 1, i) for i in lows]


def local(field, tf_density, tf_color):
    frames, depth, columns, rows = field.shape
    ny, nz = lax.axis_size("gy"), lax.axis_size("gz")
    step = 1.5 / (depth * nz)
    place = lax.axis_index("gz")
    quarter = jnp.where(place < nz // 2, place, nz - 1 - place)
    odd = jnp.stack([lax.axis_index("gy") % 2, place % 2, quarter % 2]).astype(jnp.int32)
    split = 7

    smem = pl.BlockSpec(memory_space=pltpu.SMEM)
    anywhere, vmem = pl.BlockSpec(memory_space=pl.ANY), pl.BlockSpec(memory_space=pltpu.VMEM)
    plane = jax.ShapeDtypeStruct((frames, columns, rows), jnp.float32)
    outer, second, pair, other = pl.pallas_call(
        edges_kernel,
        in_specs=[smem, anywhere],
        out_specs=[vmem] * 4,
        out_shape=[plane] * 4,
        scratch_shapes=[pltpu.VMEM(field.shape, jnp.float32), pltpu.SemaphoreType.DMA((frames,))],
        compiler_params=pltpu.CompilerParams(vmem_limit_bytes=56 * 2**20),
        name="edges",
    )(odd, field)
    z1 = lax.ppermute(pair, "gz", pairs_of(nz, 0))
    z2 = lax.ppermute(other, "gz", pairs_of(nz, 1))
    y1 = lax.ppermute(outer, "gy", pairs_of(ny, 0))
    y2 = lax.ppermute(outer, "gy", pairs_of(ny, 1))

    def render(name, start, count, *earlier):
        voxels = count * depth * columns * rows
        share = jax.ShapeDtypeStruct((4, count, 4, columns // nz, rows), jnp.float32)
        share_spec = pl.BlockSpec((4, 1, 4, columns // nz, rows), lambda f: (0, f, 0, 0, 0))
        plane_spec = pl.BlockSpec((1, columns, rows), lambda f: (f + start, 0, 0))
        return pl.pallas_call(
            functools.partial(render_kernel, step=step, start=start),
            grid=(count,),
            in_specs=[smem, smem, smem] + [plane_spec] * 5 + [anywhere] * (1 + len(earlier)),
            out_specs=[share_spec, share_spec],
            out_shape=[share, share],
            scratch_shapes=[
                pltpu.VMEM((2, depth + 3, PITCH, LANES), jnp.float32),
                pltpu.SemaphoreType.DMA((2,)),
            ],
            compiler_params=pltpu.CompilerParams(vmem_limit_bytes=52 * 2**20),
            cost_estimate=pl.CostEstimate(flops=12000 * voxels, bytes_accessed=4 * voxels, transcendentals=5 * voxels),
            name=name,
        )(odd, tf_density, tf_color, z1, z2, y1, y2, second, field, *earlier)

    def swapped(value, partner):
        return lax.ppermute(value, "gz", [(i, partner(i)) for i in range(nz)])

    def swapped_first(sent):
        return swapped(sent, lambda i: i ^ 1)

    kept_a, sent_a = render("render_a", 0, split)
    kept_b, sent_b = render("render_b", split, frames - split, kept_a)
    arrived_a, sent_b = lax.optimization_barrier((swapped_first(sent_a), sent_b))
    in_front = place % 2 == 0
    value = jnp.concatenate(
        [joined(kept_a, arrived_a, in_front), joined(kept_b, swapped_first(sent_b), in_front)], axis=1
    )
    kept, sent = halves(value, quarter // 2)
    value = joined(kept, swapped(sent, lambda i: i ^ 2), place // 2 % 2 == 0)
    kept, sent = halves(value, place // 4)
    value = joined(kept, swapped(sent, lambda i: nz - 1 - i), place < nz // 2)[0]
    return jnp.concatenate([value[:, :3], 1.0 - jnp.exp2(value[:, 3:])], axis=1)


def solution(mesh):
    placed = (P(None, "gz", None, "gy"), P(), P())
    return jax.shard_map(
        local, mesh=mesh, in_specs=placed, out_specs=P(None, None, "gz", "gy"), check_vma=False
    )
```

time: 464 us -> 74.2 us (0.16); the launches traced: 457 us -> 74 us
  other arithmetic: 307 us -> 1.93 us
  local copies, waits for them, and re-layouts: 83.1 us -> 0.93 us
  Pallas kernels: 0 us -> 33 us
  matrix products: 17.2 us -> 0 us
  waiting for transfers between devices: 27.8 us -> 21.1 us
    reduce_sum x30 -> x0, other arithmetic: 281 us -> none  [the longest x20 213 us: local_image(): colors = [jnp.sum(weight * tints[c], axis=0) for c in range(3)]]
    slice x32 -> x1, local copies, waits for them, and re-layouts: 36.7 us -> 0.01 us  [local(): return jnp.concatenate([value[:, :3], 1.0 - jnp.exp2(value[:, 3:])], axis=1)]
    pallas_call x0 -> x3, Pallas kernels: none -> 33 us  [the longest x2 26.6 us: render(): pl.pallas_call(functools.partial(render_kernel, step=step, start=start),...]
    concatenate x2, other arithmetic: 22.7 us -> 0.73 us  [the longest x1 0.66 us: local(): return jnp.concatenate([value[:, :3], 1.0 - jnp.exp2(value[:, 3:])], axis=1)]
    squeeze x13 -> x0, local copies, waits for them, and re-layouts: 18.7 us -> none  [the longest x10 18.5 us: local(): lax.map(lambda slab: local_image(slab, tf_density, tf_color, lower, step)...]
    dot_general x10 -> x0, matrix products: 17.2 us -> none  [local_image(): jnp.dot(lower, tau.reshape(depth, -1), precision=lax.Precision.HIGHEST)]
    ppermute x2 -> x0, local copies, waits for them, and re-layouts: 12.5 us -> none  [the longest x1 6.32 us: with_halo(): lax.ppermute(tail, axis, [(i, (i + 1) % count) for i in range(ends)])]
    unnamed x6 -> x8, local copies, waits for them, and re-layouts: 13.3 us -> 0.92 us
  transfers between devices with their start and end apart: 7 -> 8, of which waited for: 5 -> 5; matrix products, arithmetic and copies ran while one was open for 3% -> 0% of each run, Pallas kernels for 0% -> 12%
where the time goes in v1:
time: 74.2 us; the launch traced here: 74 us
  Pallas kernels  33 us (44%)
  waiting for transfers between devices  21.1 us (28%)
  starting transfers between devices  16.9 us (23%)
  other arithmetic  1.93 us (3%)
  local copies, waits for them, and re-layouts  0.93 us (1%)
    pallas_call x2, Pallas kernels, render(): pl.pallas_call(functools.partial(render_kernel, step=step, start=start),...  26.6 us
    ppermute x4, waiting for transfers between devices, swapped(): return lax.ppermute(value, 'gz', [(i, partner(i)) for i in range(nz)])  17.3 us
    ppermute x4, starting transfers between devices, swapped(): return lax.ppermute(value, 'gz', [(i, partner(i)) for i in range(nz)])  11.2 us
    pallas_call x1, Pallas kernels, local(): pl.pallas_call(edges_kernel, in_specs=[smem, anywhere], out_specs=[vmem]...  6.35 us
    ppermute x1, waiting for transfers between devices, local(): y2 = lax.ppermute(outer, 'gy', pairs_of(ny, 1))  3.1 us
    ppermute x1, starting transfers between devices, local(): z1 = lax.ppermute(pair, 'gz', pairs_of(nz, 0))  2 us
    ppermute x1, starting transfers between devices, local(): y2 = lax.ppermute(outer, 'gy', pairs_of(ny, 1))  1.92 us
  transfers between devices with their start and end apart: 8, of which 5 were waited for; matrix products, arithmetic and copies ran while one was open for 0% of the time, Pallas kernels for 12%

profile of v1, /device:TPU:28, one launch (start us, length us, event | category | flops | bytes accessed | tf_op | source)
XLA Modules:
  0.0 74.0 jit_solution(7937013115533125419)
XLA Ops:
  0.0 0.0 copy-start.2
  0.0 0.0 copy-start.3
  0.0 0.7 pad_add_fusion.odd_ref
  0.7 0.0 copy-start
  0.7 6.3 %edges.1 = (f32[10,32,128]{2,1,0:T(8,128)}, f32[10,32,128]{2,1,0:T(8,128)}, f32[10,32,128]{2,1,0:T(8,128)}, f32[10,32,128]{2,1,0:T(8,128)}) custom-call(s32[3]{0:T(128)} %pad_add_fusion.odd_ref, f32[10,64,32,128]{3,2,1,0:T(8,128)} %field_ref.5), custom_call_target="tpu_custom_call" | custom-call | tf_op jit(solution)/shard_map/edges/pallas_call | solution.py:213
  7.0 2.0 %collective-permute-start = (f32[10,32,128]{2,1,0:T(8,128)}, f32[10,32,128]{2,1,0:T(8,128)S(1)}, u32[]{:S(2)}, u32[]{:S(2)}) collective-permute-start(f32[10,32,128]{2,1,0:T(8,128)} %get-tuple-element.15), channel_id=1, source_target_pairs={{0,1},{2,3},{4,5},{6,7},{1,0},{3,2},{5,4},{7,6},{8,9},{10,11},{12,... | collective-permute-start | bytes 491528 | tf_op jit(solution)/shard_map/ppermute | solution.py:222
  9.0 0.7 collective-permute-start.1
  9.7 1.9 %collective-permute-start.3 = (f32[10,32,128]{2,1,0:T(8,128)}, f32[10,32,128]{2,1,0:T(8,128)S(1)}, u32[]{:S(2)}, u32[]{:S(2)}) collective-permute-start(f32[10,32,128]{2,1,0:T(8,128)} %get-tuple-element.17), channel_id=1, source_target_pairs={{8,16},{24,32},{40,48},{56,64},{72,80},{88,96},{104,112},{120,128}... | collective-permute-start | bytes 491528 | tf_op jit(solution)/shard_map/ppermute | solution.py:225
  11.6 1.0 %collective-permute-start.2 = (f32[10,32,128]{2,1,0:T(8,128)}, f32[10,32,128]{2,1,0:T(8,128)S(1)}, u32[]{:S(2)}, u32[]{:S(2)}) collective-permute-start(f32[10,32,128]{2,1,0:T(8,128)} %get-tuple-element.17), channel_id=1, source_target_pairs={{0,8},{16,24},{32,40},{48,56},{64,72},{80,88},{96,104},{112,120},{... | collective-permute-start | bytes 491528 | tf_op jit(solution)/shard_map/ppermute | solution.py:224
  12.7 0.8 %collective-permute-done.z1_ref = f32[10,32,128]{2,1,0:T(8,128)S(1)} collective-permute-done((f32[10,32,128]{2,1,0:T(8,128)}, f32[10,32,128]{2,1,0:T(8,128)S(1)}, u32[]{:S(2)}, u32[]{:S(2)}) %collective-permute-start) | collective-permute-done | bytes 163872 | tf_op jit(solution)/shard_map/ppermute | solution.py:222
  13.4 0.0 collective-permute-done.1.z2_ref
  13.4 3.1 %collective-permute-done.3.y2_ref = f32[10,32,128]{2,1,0:T(8,128)S(1)} collective-permute-done((f32[10,32,128]{2,1,0:T(8,128)}, f32[10,32,128]{2,1,0:T(8,128)S(1)}, u32[]{:S(2)}, u32[]{:S(2)}) %collective-permute-start.3) | collective-permute-done | bytes 163872 | tf_op jit(solution)/shard_map/ppermute | solution.py:225
  16.5 0.0 collective-permute-done.2.y1_ref
  16.5 0.0 copy-done.2
  16.6 0.0 copy-done.3
  16.6 0.0 copy-done
  16.6 0.0 copy-start.1
  16.6 0.9 %copy-done.1 = f32[10,32,128]{2,1,0:T(8,128)S(1)} copy-done((f32[10,32,128]{2,1,0:T(8,128)S(1)}, f32[10,32,128]{2,1,0:T(8,128)}, u32[]{:S(2)}) %copy-start.1) | copy-done | bytes 163864
  17.5 17.9 %render_a.1 = (f32[4,7,4,4,128]{4,3,2,1,0:T(4,128)S(1)}, f32[4,7,4,4,128]{4,3,2,1,0:T(4,128)S(1)}) custom-call(s32[3]{0:T(128)S(1)} %copy-done, f32[8]{0:T(128)S(1)} %copy-done.3, f32[3,8]{1,0:T(4,128)S(1)} %copy-done.2, f32[10,32,128]{2,1,0:T(8,128)S(1)} %collective-permute-done.z1_ref, f32[10,32,128]{2,1,0:T(8,128)S(1)} %collective-permute-done.1.z2_ref, ...), custom_call_target="tpu_custom_call" | custom-call | flops 22020096000 | bytes 7340032 | tf_op jit(solution)/shard_map/render_a/pallas_call | solution.py:232
  35.4 5.2 %collective-permute-start.4 = (f32[4,7,4,4,128]{4,3,2,1,0:T(4,128)S(1)}, f32[4,7,4,4,128]{4,3,2,1,0:T(4,128)S(1)}, u32[]{:S(2)}, u32[]{:S(2)}) collective-permute-start(f32[4,7,4,4,128]{4,3,2,1,0:T(4,128)S(1)} %get-tuple-element.20), channel_id=1, source_target_pairs={{0,1},{1,0},{2,3},{3,2},{4,5},{5,4},{6,7},{7,6},{8,9},{9,8},{10,11... | collective-permute-start | bytes 688136 | tf_op jit(solution)/shard_map/ppermute | solution.py:248
  40.6 8.7 %render_b.1 = (f32[4,3,4,4,128]{4,3,2,1,0:T(4,128)S(1)}, f32[4,3,4,4,128]{4,3,2,1,0:T(4,128)S(1)}) custom-call(s32[3]{0:T(128)S(1)} %copy-done, f32[8]{0:T(128)S(1)} %copy-done.3, f32[3,8]{1,0:T(4,128)S(1)} %copy-done.2, f32[10,32,128]{2,1,0:T(8,128)S(1)} %collective-permute-done.z1_ref, f32[10,32,128]{2,1,0:T(8,128)S(1)} %collective-permute-done.1.z2_ref, ...), custom_call_target="tpu_custom_call" | custom-call | flops 9437184000 | bytes 3145728 | tf_op jit(solution)/shard_map/render_b/pallas_call | solution.py:232
  49.3 0.0 collective-permute-done.4
  49.3 0.1 collective-permute-start.5
  49.5 0.1 fusion
  49.6 5.3 %collective-permute-done.5 = f32[4,3,4,4,128]{4,3,2,1,0:T(4,128)S(1)} collective-permute-done((f32[4,3,4,4,128]{4,3,2,1,0:T(4,128)S(1)}, f32[4,3,4,4,128]{4,3,2,1,0:T(4,128)S(1)}, u32[]{:S(2)}, u32[]{:S(2)}) %collective-permute-start.5) | collective-permute-done | bytes 98336 | tf_op jit(solution)/shard_map/ppermute | solution.py:248
  55.0 0.1 maximum_maximum_fusion
  55.1 3.7 %collective-permute-start.6 = (f32[2,10,4,4,128]{4,3,2,1,0:T(4,128)S(1)}, f32[2,10,4,4,128]{4,3,2,1,0:T(4,128)S(1)}, u32[]{:S(2)}, u32[]{:S(2)}) collective-permute-start(f32[2,10,4,4,128]{4,3,2,1,0:T(4,128)S(1)} %slice_select_fusion), channel_id=1, source_target_pairs={{0,2},{1,3},{2,0},{3,1},{4,6},{5,7},{6,4},{7,5},{8,10},{9,11},{10,... | collective-permute-start | bytes 491528 | tf_op jit(solution)/shard_map/ppermute | solution.py:248
  58.8 7.3 %collective-permute-done.6 = f32[2,10,4,4,128]{4,3,2,1,0:T(4,128)S(1)} collective-permute-done((f32[2,10,4,4,128]{4,3,2,1,0:T(4,128)S(1)}, f32[2,10,4,4,128]{4,3,2,1,0:T(4,128)S(1)}, u32[]{:S(2)}, u32[]{:S(2)}) %collective-permute-start.6) | collective-permute-done | bytes 163872 | tf_op jit(solution)/shard_map/ppermute | solution.py:248
  66.1 0.1 broadcast_select_fusion.3
  66.3 2.3 %collective-permute-start.7 = (f32[1,10,4,4,128]{4,3,2,1,0:T(4,128)S(1)}, f32[1,10,4,4,128]{4,3,2,1,0:T(4,128)S(1)}, u32[]{:S(2)}, u32[]{:S(2)}) collective-permute-start(f32[1,10,4,4,128]{4,3,2,1,0:T(4,128)S(1)} %broadcast_select_fusion.6), channel_id=1, source_target_pairs={{0,7},{1,6},{2,5},{3,4},{4,3},{5,2},{6,1},{7,0},{8,15},{9,14},{10,... | collective-permute-start | bytes 245768 | tf_op jit(solution)/shard_map/ppermute | solution.py:248
  68.6 4.6 %collective-permute-done.7 = f32[1,10,4,4,128]{4,3,2,1,0:T(4,128)S(1)} collective-permute-done((f32[1,10,4,4,128]{4,3,2,1,0:T(4,128)S(1)}, f32[1,10,4,4,128]{4,3,2,1,0:T(4,128)S(1)}, u32[]{:S(2)}, u32[]{:S(2)}) %collective-permute-start.7) | collective-permute-done | bytes 81952 | tf_op jit(solution)/shard_map/ppermute | solution.py:248
  73.4 0.7 pad_maximum_fusion.1
  (15 shorter events, 0.4 us)
Async XLA Ops:
  0.0 16.5 %copy-start.2 = (f32[3,8]{1,0:T(4,128)S(1)}, f32[3,8]{1,0:T(4,128)}, u32[]{:S(2)}) copy-start(f32[3,8]{1,0:T(4,128)} %color_ref.3) | copy-start | bytes 292
  0.0 16.6 %copy-start.3 = (f32[8]{0:T(128)S(1)}, f32[8]{0:T(128)}, u32[]{:S(2)}) copy-start(f32[8]{0:T(128)} %density_ref.3) | copy-start | bytes 100
  0.7 15.9 %copy-start = (s32[3]{0:T(128)S(1)}, s32[3]{0:T(128)}, u32[]{:S(2)}) copy-start(s32[3]{0:T(128)} %pad_add_fusion.odd_ref) | copy-start | bytes 40
  7.0 6.4 %collective-permute-start = (f32[10,32,128]{2,1,0:T(8,128)}, f32[10,32,128]{2,1,0:T(8,128)S(1)}, u32[]{:S(2)}, u32[]{:S(2)}) collective-permute-start(f32[10,32,128]{2,1,0:T(8,128)} %get-tuple-element.15), channel_id=1, source_target_pairs={{0,1},{2,3},{4,5},{6,7},{1,0},{3,2},{5,4},{7,6},{8,9},{10,11},{12,... | collective-permute-start | bytes 491528 | tf_op jit(solution)/shard_map/ppermute | solution.py:222
  9.0 4.4 %collective-permute-start.1 = (f32[10,32,128]{2,1,0:T(8,128)}, f32[10,32,128]{2,1,0:T(8,128)S(1)}, u32[]{:S(2)}, u32[]{:S(2)}) collective-permute-start(f32[10,32,128]{2,1,0:T(8,128)} %get-tuple-element.16), channel_id=1, source_target_pairs={{1,2},{3,4},{5,6},{2,1},{4,3},{6,5},{9,10},{11,12},{13,14},{10,9},... | collective-permute-start | bytes 491528 | tf_op jit(solution)/shard_map/ppermute | solution.py:223
  9.7 6.8 %collective-permute-start.3 = (f32[10,32,128]{2,1,0:T(8,128)}, f32[10,32,128]{2,1,0:T(8,128)S(1)}, u32[]{:S(2)}, u32[]{:S(2)}) collective-permute-start(f32[10,32,128]{2,1,0:T(8,128)} %get-tuple-element.17), channel_id=1, source_target_pairs={{8,16},{24,32},{40,48},{56,64},{72,80},{88,96},{104,112},{120,128}... | collective-permute-start | bytes 491528 | tf_op jit(solution)/shard_map/ppermute | solution.py:225
  11.6 4.9 %collective-permute-start.2 = (f32[10,32,128]{2,1,0:T(8,128)}, f32[10,32,128]{2,1,0:T(8,128)S(1)}, u32[]{:S(2)}, u32[]{:S(2)}) collective-permute-start(f32[10,32,128]{2,1,0:T(8,128)} %get-tuple-element.17), channel_id=1, source_target_pairs={{0,8},{16,24},{32,40},{48,56},{64,72},{80,88},{96,104},{112,120},{... | collective-permute-start | bytes 491528 | tf_op jit(solution)/shard_map/ppermute | solution.py:224
  16.6 0.9 %copy-start.1 = (f32[10,32,128]{2,1,0:T(8,128)S(1)}, f32[10,32,128]{2,1,0:T(8,128)}, u32[]{:S(2)}) copy-start(f32[10,32,128]{2,1,0:T(8,128)} %get-tuple-element.18.second_ref) | copy-start | bytes 491524
  35.4 13.9 %collective-permute-start.4 = (f32[4,7,4,4,128]{4,3,2,1,0:T(4,128)S(1)}, f32[4,7,4,4,128]{4,3,2,1,0:T(4,128)S(1)}, u32[]{:S(2)}, u32[]{:S(2)}) collective-permute-start(f32[4,7,4,4,128]{4,3,2,1,0:T(4,128)S(1)} %get-tuple-element.20), channel_id=1, source_target_pairs={{0,1},{1,0},{2,3},{3,2},{4,5},{5,4},{6,7},{7,6},{8,9},{9,8},{10,11... | collective-permute-start | bytes 688136 | tf_op jit(solution)/shard_map/ppermute | solution.py:248
  49.3 5.6 %collective-permute-start.5 = (f32[4,3,4,4,128]{4,3,2,1,0:T(4,128)S(1)}, f32[4,3,4,4,128]{4,3,2,1,0:T(4,128)S(1)}, u32[]{:S(2)}, u32[]{:S(2)}) collective-permute-start(f32[4,3,4,4,128]{4,3,2,1,0:T(4,128)S(1)} %get-tuple-element.24), channel_id=1, source_target_pairs={{0,1},{1,0},{2,3},{3,2},{4,5},{5,4},{6,7},{7,6},{8,9},{9,8},{10,11... | collective-permute-start | bytes 294920 | tf_op jit(solution)/shard_map/ppermute | solution.py:248
  55.1 11.0 %collective-permute-start.6 = (f32[2,10,4,4,128]{4,3,2,1,0:T(4,128)S(1)}, f32[2,10,4,4,128]{4,3,2,1,0:T(4,128)S(1)}, u32[]{:S(2)}, u32[]{:S(2)}) collective-permute-start(f32[2,10,4,4,128]{4,3,2,1,0:T(4,128)S(1)} %slice_select_fusion), channel_id=1, source_target_pairs={{0,2},{1,3},{2,0},{3,1},{4,6},{5,7},{6,4},{7,5},{8,10},{9,11},{10,... | collective-permute-start | bytes 491528 | tf_op jit(solution)/shard_map/ppermute | solution.py:248
  66.3 6.9 %collective-permute-start.7 = (f32[1,10,4,4,128]{4,3,2,1,0:T(4,128)S(1)}, f32[1,10,4,4,128]{4,3,2,1,0:T(4,128)S(1)}, u32[]{:S(2)}, u32[]{:S(2)}) collective-permute-start(f32[1,10,4,4,128]{4,3,2,1,0:T(4,128)S(1)} %broadcast_select_fusion.6), channel_id=1, source_target_pairs={{0,7},{1,6},{2,5},{3,4},{4,3},{5,2},{6,1},{7,0},{8,15},{9,14},{10,... | collective-permute-start | bytes 245768 | tf_op jit(solution)/shard_map/ppermute | solution.py:248

commit v2 on v1

--- a/solution.py
+++ b/solution.py
@@ -21,10 +21,10 @@
 PITCH = 40
 
 
-def edges_kernel(odd_ref, field_ref, outer_ref, second_ref, pair_ref, next_ref, cells, sems):
+def edges_kernel(field_ref, outer_ref, second_ref, pair_ref, next_ref, cells, sems):
     frames, depth, columns = field_ref.shape[:3]
     lane = lax.broadcasted_iota(jnp.int32, (TILE, LANES), 1)
-    odd_z = odd_ref[1] == 1
+    odd_z = lax.axis_index("gz") % 2 == 1
     spans = [slice(t, t + TILE) for t in range(0, columns, TILE)]
 
     def load(f):
@@ -55,8 +55,11 @@
     lax.fori_loop(0, frames, one_frame, 0)
 
 
+def quarter_of(place, count):
+    return jnp.where(place < count // 2, place, count - 1 - place)
+
+
 def render_kernel(
-    odd_ref,
     density_ref,
     color_ref,
     z1_ref,
@@ -70,51 +73,38 @@
     start,
 ):
     kept_ref, sent_ref, cells, sems = rest[-4:]
-    frame, frames = pl.program_id(0), pl.num_programs(0)
     depth, columns = field_ref.shape[1], field_ref.shape[2]
+    frames = kept_ref.shape[1]
     tiles = columns // TILE
-    slot = lax.rem(frame, 2)
-
-    def load(which, into):
+
+    def load(frame, into, t):
         return pltpu.make_async_copy(
-            field_ref.at[start + which], cells.at[into, pl.ds(1, depth), pl.ds(TILE, columns), :], sems.at[into]
+            field_ref.at[start + frame, :, pl.ds(t * TILE, TILE), :],
+            cells.at[into, pl.ds(1, depth), pl.ds((t + 1) * TILE, TILE), :],
+            sems.at[into, t],
         )
 
-    @pl.when(frame == 0)
-    def _():
-        load(0, 0).start()
-        for into in range(2):
-            for plane in range(depth + 3):
-                cells[into, plane, 0:TILE, :] = jnp.zeros((TILE, LANES), jnp.float32)
-
-    @pl.when(frame + 1 < frames)
-    def _():
-        load(frame + 1, 1 - slot).start()
-
-    odd_y, odd_z, late = odd_ref[0] == 1, odd_ref[1] == 1, odd_ref[2]
+    for t in range(tiles):
+        load(0, 0, t).start()
+    for into in range(2):
+        for plane in range(depth + 3):
+            cells[into, plane, 0:TILE, :] = jnp.zeros((TILE, LANES), jnp.float32)
+
+    place = lax.axis_index("gz")
+    odd_y, odd_z, late = lax.axis_index("gy") % 2 == 1, place % 2 == 1, quarter_of(place, lax.axis_size("gz")) % 2
     lane = lax.broadcasted_iota(jnp.int32, (TILE, LANES), 1)
     even_lane = (lane & 1) == 0
     edge_lane = (lane == 0) | (lane == LANES - 1)
-
     rows = cells.reshape(2 * cells.shape[1] * PITCH, LANES)
-    first = slot * (cells.shape[1] * PITCH) + TILE
-
-    for t in range(tiles):
-        here = slice(t * TILE, (t + 1) * TILE)
-        a, b = z1_ref[0, here, :], z2_ref[0, here, :]
-        cells[slot, 0, TILE + t * TILE : TILE + (t + 1) * TILE, :] = jnp.where(odd_z, a, b)
-        cells[slot, depth + 1, TILE + t * TILE : TILE + (t + 1) * TILE, :] = jnp.where(odd_z, b, a)
-
     scale = [-LOG2E * step * FALL[j] for j in range(BUMPS)]
     dens = [jnp.full((TILE, LANES), density_ref[j] * scale[j], jnp.float32) for j in range(BUMPS)]
-    load(frame, slot).wait()
-
-    def one_tile(t, _):
-        top = first + t * TILE
+
+    def one_tile(frame, slot, t):
+        top = slot * (cells.shape[1] * PITCH) + TILE + t * TILE
         here = pl.ds(pl.multiple_of(t * TILE, TILE), TILE)
-        a, b = y1_ref[0, here, :], y2_ref[0, here, :]
+        a, b = y1_ref[start + frame, here, :], y2_ref[start + frame, here, :]
         left, right = jnp.where(odd_y, a, b), jnp.where(odd_y, b, a)
-        second = second_ref[0, here, :]
+        second = second_ref[start + frame, here, :]
         rim = jnp.where(
             even_lane,
             pltpu.roll(right, LANES - 1, 1) - pltpu.roll(second, 1, 1),
@@ -174,11 +164,36 @@
         keep_first = late == jnp.where(t >= 2, 1, 0)
         share = jnp.where(t == 0, 0, jnp.where(t == 1, 2, jnp.where(t == 2, 3, 1)))
         for c in range(4):
-            kept_ref[share, 0, c, :, :] = jnp.where(keep_first, parts[c][0:4], parts[c][4:8])
-            sent_ref[share, 0, c, :, :] = jnp.where(keep_first, parts[c][4:8], parts[c][0:4])
+            kept_ref[share, frame, c, :, :] = jnp.where(keep_first, parts[c][0:4], parts[c][4:8])
+            sent_ref[share, frame, c, :, :] = jnp.where(keep_first, parts[c][4:8], parts[c][0:4])
+
+    def one_frame(frame, _):
+        slot = lax.rem(frame, 2)
+
+        @pl.when(frame + 1 < frames)
+        def _():
+            for t in range(tiles):
+                load(frame + 1, 1 - slot, t).start()
+
+        for t in range(tiles):
+            here, there = slice(t * TILE, (t + 1) * TILE), slice((t + 1) * TILE, (t + 2) * TILE)
+            a, b = z1_ref[start + frame, here, :], z2_ref[start + frame, here, :]
+            cells[slot, 0, there, :] = jnp.where(odd_z, a, b)
+            cells[slot, depth + 1, there, :] = jnp.where(odd_z, b, a)
+        load(frame, slot, 0).wait()
+
+        def with_next(t, _):
+            @pl.when(t + 1 < tiles)
+            def _():
+                load(frame, slot, t + 1).wait()
+
+            one_tile(frame, slot, t)
+            return 0
+
+        lax.fori_loop(0, tiles, with_next, 0)
         return 0
 
-    lax.fori_loop(0, tiles, one_tile, 0)
+    lax.fori_loop(0, frames, one_frame, 0)
 
 
 def joined(kept, arrived, in_front):
@@ -203,8 +218,7 @@
     ny, nz = lax.axis_size("gy"), lax.axis_size("gz")
     step = 1.5 / (depth * nz)
     place = lax.axis_index("gz")
-    quarter = jnp.where(place < nz // 2, place, nz - 1 - place)
-    odd = jnp.stack([lax.axis_index("gy") % 2, place % 2, quarter % 2]).astype(jnp.int32)
+    late = quarter_of(place, nz) // 2
     split = 7
 
     smem = pl.BlockSpec(memory_space=pltpu.SMEM)
@@ -212,13 +226,13 @@
     plane = jax.ShapeDtypeStruct((frames, columns, rows), jnp.float32)
     outer, second, pair, other = pl.pallas_call(
         edges_kernel,
-        in_specs=[smem, anywhere],
+        in_specs=[anywhere],
         out_specs=[vmem] * 4,
         out_shape=[plane] * 4,
         scratch_shapes=[pltpu.VMEM(field.shape, jnp.float32), pltpu.SemaphoreType.DMA((frames,))],
-        compiler_params=pltpu.CompilerParams(vmem_limit_bytes=56 * 2**20),
+        compiler_params=pltpu.CompilerParams(vmem_limit_bytes=52 * 2**20),
         name="edges",
-    )(odd, field)
+    )(field)
     z1 = lax.ppermute(pair, "gz", pairs_of(nz, 0))
     z2 = lax.ppermute(other, "gz", pairs_of(nz, 1))
     y1 = lax.ppermute(outer, "gy", pairs_of(ny, 0))
@@ -227,22 +241,19 @@
     def render(name, start, count, *earlier):
         voxels = count * depth * columns * rows
         share = jax.ShapeDtypeStruct((4, count, 4, columns // nz, rows), jnp.float32)
-        share_spec = pl.BlockSpec((4, 1, 4, columns // nz, rows), lambda f: (0, f, 0, 0, 0))
-        plane_spec = pl.BlockSpec((1, columns, rows), lambda f: (f + start, 0, 0))
         return pl.pallas_call(
             functools.partial(render_kernel, step=step, start=start),
-            grid=(count,),
-            in_specs=[smem, smem, smem] + [plane_spec] * 5 + [anywhere] * (1 + len(earlier)),
-            out_specs=[share_spec, share_spec],
+            in_specs=[smem, smem] + [vmem] * 5 + [anywhere] * (1 + len(earlier)),
+            out_specs=[vmem, vmem],
             out_shape=[share, share],
             scratch_shapes=[
                 pltpu.VMEM((2, depth + 3, PITCH, LANES), jnp.float32),
-                pltpu.SemaphoreType.DMA((2,)),
+                pltpu.SemaphoreType.DMA((2, columns // TILE)),
             ],
             compiler_params=pltpu.CompilerParams(vmem_limit_bytes=52 * 2**20),
             cost_estimate=pl.CostEstimate(flops=12000 * voxels, bytes_accessed=4 * voxels, transcendentals=5 * voxels),
             name=name,
-        )(odd, tf_density, tf_color, z1, z2, y1, y2, second, field, *earlier)
+        )(tf_density, tf_color, z1, z2, y1, y2, second, field, *earlier)
 
     def swapped(value, partner):
         return lax.ppermute(value, "gz", [(i, partner(i)) for i in range(nz)])
@@ -253,12 +264,12 @@
     kept_a, sent_a = render("render_a", 0, split)
     kept_b, sent_b = render("render_b", split, frames - split, kept_a)
     arrived_a, sent_b = lax.optimization_barrier((swapped_first(sent_a), sent_b))
-    in_front = place % 2 == 0
-    value = jnp.concatenate(
-        [joined(kept_a, arrived_a, in_front), joined(kept_b, swapped_first(sent_b), in_front)], axis=1
-    )
-    kept, sent = halves(value, quarter // 2)
-    value = joined(kept, swapped(sent, lambda i: i ^ 2), place // 2 % 2 == 0)
+
+    def second_join(kept, arrived):
+        kept, sent = halves(joined(kept, arrived, place % 2 == 0), late)
+        return joined(kept, swapped(sent, lambda i: i ^ 2), place // 2 % 2 == 0)
+
+    value = jnp.concatenate([second_join(kept_a, arrived_a), second_join(kept_b, swapped_first(sent_b))], axis=1)
     kept, sent = halves(value, place // 4)
     value = joined(kept, swapped(sent, lambda i: nz - 1 - i), place < nz // 2)[0]
     return jnp.concatenate([value[:, :3], 1.0 - jnp.exp2(value[:, 3:])], axis=1)

time: 74.2 us -> 67.4 us (0.908)
  waiting for transfers between devices: 21.1 us -> 16 us
  Pallas kernels: 33 us -> 30.8 us
  starting transfers between devices: 16.9 us -> 18.9 us
  local copies, waits for them, and re-layouts: 0.93 us -> 0.02 us
    ppermute x4 -> x5, waiting for transfers between devices: 17.3 us -> 12.1 us  [swapped(): return lax.ppermute(value, 'gz', [(i, partner(i)) for i in range(nz)])]
    ppermute x4 -> x5, starting transfers between devices: 11.2 us -> 13.4 us  [swapped(): return lax.ppermute(value, 'gz', [(i, partner(i)) for i in range(nz)])]
    pallas_call x1, Pallas kernels: 6.35 us -> 4.85 us  [local(): pl.pallas_call(edges_kernel, in_specs=[anywhere], out_specs=[vmem] * 4, o...]
    ppermute x1, starting transfers between devices: 1.05 us -> 0.09 us  [local(): y1 = lax.ppermute(outer, 'gy', pairs_of(ny, 0))]
    unnamed x8 -> x4, local copies, waits for them, and re-layouts: 0.92 us -> 0.01 us
    ppermute x1, starting transfers between devices: 1.92 us -> 2.74 us  [local(): y2 = lax.ppermute(outer, 'gy', pairs_of(ny, 1))]
  transfers between devices with their start and end apart: 8 -> 9, of which waited for: 5 -> 5; matrix products, arithmetic and copies ran while one was open for 0% -> 1% of each run, Pallas kernels for 12% -> 13%
where the time goes in v2:
time: 67.4 us; the launch traced here: 67.3 us
  Pallas kernels  30.8 us (46%)
  starting transfers between devices  18.9 us (28%)
  waiting for transfers between devices  16 us (24%)
  other arithmetic  1.26 us (2%)
    pallas_call x2, Pallas kernels, render(): pl.pallas_call(functools.partial(render_kernel, step=step, start=start),...  26 us
    ppermute x5, starting transfers between devices, swapped(): return lax.ppermute(value, 'gz', [(i, partner(i)) for i in range(nz)])  13.4 us
    ppermute x5, waiting for transfers between devices, swapped(): return lax.ppermute(value, 'gz', [(i, partner(i)) for i in range(nz)])  12.1 us
    pallas_call x1, Pallas kernels, local(): pl.pallas_call(edges_kernel, in_specs=[anywhere], out_specs=[vmem] * 4, o...  4.85 us
    ppermute x1, waiting for transfers between devices, local(): y2 = lax.ppermute(outer, 'gy', pairs_of(ny, 1))  3.2 us
    ppermute x1, starting transfers between devices, local(): y2 = lax.ppermute(outer, 'gy', pairs_of(ny, 1))  2.74 us
    ppermute x1, starting transfers between devices, local(): z1 = lax.ppermute(pair, 'gz', pairs_of(nz, 0))  2 us
  transfers between devices with their start and end apart: 9, of which 5 were waited for; matrix products, arithmetic and copies ran while one was open for 1% of the time, Pallas kernels for 13%

profile of v2, /device:TPU:28, one launch (start us, length us, event | category | flops | bytes accessed | tf_op | source)
XLA Modules:
  0.0 67.3 jit_solution(9323502038664602392)
XLA Ops:
  0.0 0.0 copy-start.1
  0.0 0.0 copy-start
  0.0 4.8 %edges.1 = (f32[10,32,128]{2,1,0:T(8,128)S(1)}, f32[10,32,128]{2,1,0:T(8,128)S(1)}, f32[10,32,128]{2,1,0:T(8,128)S(1)}, f32[10,32,128]{2,1,0:T(8,128)S(1)}) custom-call(f32[10,64,32,128]{3,2,1,0:T(8,128)} %field_ref.5), custom_call_target="tpu_custom_call" | custom-call | tf_op jit(solution)/shard_map/edges/pallas_call | solution.py:227
  4.9 2.0 %collective-permute-start = (f32[10,32,128]{2,1,0:T(8,128)S(1)}, f32[10,32,128]{2,1,0:T(8,128)S(1)}, u32[]{:S(2)}, u32[]{:S(2)}) collective-permute-start(f32[10,32,128]{2,1,0:T(8,128)S(1)} %get-tuple-element.15), channel_id=1, source_target_pairs={{0,1},{2,3},{4,5},{6,7},{1,0},{3,2},{5,4},{7,6},{8,9},{10,11},{12,... | collective-permute-start | bytes 491528 | tf_op jit(solution)/shard_map/ppermute | solution.py:236
  6.9 0.7 collective-permute-start.1
  7.5 0.1 collective-permute-start.2
  7.6 2.7 %collective-permute-start.3 = (f32[10,32,128]{2,1,0:T(8,128)S(1)}, f32[10,32,128]{2,1,0:T(8,128)S(1)}, u32[]{:S(2)}, u32[]{:S(2)}) collective-permute-start(f32[10,32,128]{2,1,0:T(8,128)S(1)} %get-tuple-element.17), channel_id=1, source_target_pairs={{8,16},{24,32},{40,48},{56,64},{72,80},{88,96},{104,112},{120,128}... | collective-permute-start | bytes 491528 | tf_op jit(solution)/shard_map/ppermute | solution.py:239
  10.4 0.6 collective-permute-done.z1_ref
  11.1 0.0 collective-permute-done.1.z2_ref
  11.1 0.0 collective-permute-done.2.y1_ref
  11.1 3.2 %collective-permute-done.3.y2_ref = f32[10,32,128]{2,1,0:T(8,128)S(1)} collective-permute-done((f32[10,32,128]{2,1,0:T(8,128)S(1)}, f32[10,32,128]{2,1,0:T(8,128)S(1)}, u32[]{:S(2)}, u32[]{:S(2)}) %collective-permute-start.3) | collective-permute-done | bytes 163872 | tf_op jit(solution)/shard_map/ppermute | solution.py:239
  14.3 0.0 copy-done.1
  14.3 0.0 copy-done
  14.3 17.5 %render_a.1 = (f32[4,7,4,4,128]{4,3,2,1,0:T(4,128)S(1)}, f32[4,7,4,4,128]{4,3,2,1,0:T(4,128)S(1)}) custom-call(f32[8]{0:T(128)S(1)} %copy-done.1, f32[3,8]{1,0:T(4,128)S(1)} %copy-done, f32[10,32,128]{2,1,0:T(8,128)S(1)} %collective-permute-done.z1_ref, f32[10,32,128]{2,1,0:T(8,128)S(1)} %collective-permute-done.1.z2_ref, ...), custom_call_target="tpu_custom_call" | custom-call | flops 22020096000 | bytes 7340032 | tf_op jit(solution)/shard_map/render_a/pallas_call | solution.py:244
  31.8 5.2 %collective-permute-start.4 = (f32[4,7,4,4,128]{4,3,2,1,0:T(4,128)S(1)}, f32[4,7,4,4,128]{4,3,2,1,0:T(4,128)S(1)}, u32[]{:S(2)}, u32[]{:S(2)}) collective-permute-start(f32[4,7,4,4,128]{4,3,2,1,0:T(4,128)S(1)} %get-tuple-element.20), channel_id=1, source_target_pairs={{0,1},{1,0},{2,3},{3,2},{4,5},{5,4},{6,7},{7,6},{8,9},{9,8},{10,11... | collective-permute-start | bytes 688136 | tf_op jit(solution)/shard_map/ppermute | solution.py:259
  37.0 8.4 %render_b.1 = (f32[4,3,4,4,128]{4,3,2,1,0:T(4,128)S(1)}, f32[4,3,4,4,128]{4,3,2,1,0:T(4,128)S(1)}) custom-call(f32[8]{0:T(128)S(1)} %copy-done.1, f32[3,8]{1,0:T(4,128)S(1)} %copy-done, f32[10,32,128]{2,1,0:T(8,128)S(1)} %collective-permute-done.z1_ref, f32[10,32,128]{2,1,0:T(8,128)S(1)} %collective-permute-done.1.z2_ref, ...), custom_call_target="tpu_custom_call" | custom-call | flops 9437184000 | bytes 3145728 | tf_op jit(solution)/shard_map/render_b/pallas_call | solution.py:244
  45.4 0.0 collective-permute-done.4
  45.4 0.1 collective-permute-start.6
  45.6 0.1 fusion
  45.7 3.7 %collective-permute-start.5 = (f32[2,7,4,4,128]{4,3,2,1,0:T(4,128)S(1)}, f32[2,7,4,4,128]{4,3,2,1,0:T(4,128)S(1)}, u32[]{:S(2)}, u32[]{:S(2)}) collective-permute-start(f32[2,7,4,4,128]{4,3,2,1,0:T(4,128)S(1)} %broadcast_select_fusion.2), channel_id=1, source_target_pairs={{0,2},{1,3},{2,0},{3,1},{4,6},{5,7},{6,4},{7,5},{8,10},{9,11},{10,... | collective-permute-start | bytes 344072 | tf_op jit(solution)/shard_map/ppermute | solution.py:259
  49.4 0.7 %collective-permute-done.6 = f32[4,3,4,4,128]{4,3,2,1,0:T(4,128)S(1)} collective-permute-done((f32[4,3,4,4,128]{4,3,2,1,0:T(4,128)S(1)}, f32[4,3,4,4,128]{4,3,2,1,0:T(4,128)S(1)}, u32[]{:S(2)}, u32[]{:S(2)}) %collective-permute-start.6) | collective-permute-done | bytes 98336 | tf_op jit(solution)/shard_map/ppermute | solution.py:259
  50.2 3.7 %collective-permute-start.7 = (f32[2,3,4,4,128]{4,3,2,1,0:T(4,128)S(1)}, f32[2,3,4,4,128]{4,3,2,1,0:T(4,128)S(1)}, u32[]{:S(2)}, u32[]{:S(2)}) collective-permute-start(f32[2,3,4,4,128]{4,3,2,1,0:T(4,128)S(1)} %broadcast_select_fusion.10), channel_id=1, source_target_pairs={{0,2},{1,3},{2,0},{3,1},{4,6},{5,7},{6,4},{7,5},{8,10},{9,11},{10,... | collective-permute-start | bytes 147464 | tf_op jit(solution)/shard_map/ppermute | solution.py:259
  53.9 0.0 collective-permute-done.5
  53.9 0.1 broadcast_select_fusion.5
  54.1 4.7 %collective-permute-done.7 = f32[2,3,4,4,128]{4,3,2,1,0:T(4,128)S(1)} collective-permute-done((f32[2,3,4,4,128]{4,3,2,1,0:T(4,128)S(1)}, f32[2,3,4,4,128]{4,3,2,1,0:T(4,128)S(1)}, u32[]{:S(2)}, u32[]{:S(2)}) %collective-permute-start.7) | collective-permute-done | bytes 49184 | tf_op jit(solution)/shard_map/ppermute | solution.py:259
  58.9 0.8 %collective-permute-start.8 = (f32[1,10,4,4,128]{4,3,2,1,0:T(4,128)S(1)}, f32[1,10,4,4,128]{4,3,2,1,0:T(4,128)S(1)}, u32[]{:S(2)}, u32[]{:S(2)}) collective-permute-start(f32[1,10,4,4,128]{4,3,2,1,0:T(4,128)S(1)} %slice_select_fusion), channel_id=1, source_target_pairs={{0,7},{1,6},{2,5},{3,4},{4,3},{5,2},{6,1},{7,0},{8,15},{9,14},{10,... | collective-permute-start | bytes 245768 | tf_op jit(solution)/shard_map/ppermute | solution.py:259
  59.8 6.7 %collective-permute-done.8 = f32[1,10,4,4,128]{4,3,2,1,0:T(4,128)S(1)} collective-permute-done((f32[1,10,4,4,128]{4,3,2,1,0:T(4,128)S(1)}, f32[1,10,4,4,128]{4,3,2,1,0:T(4,128)S(1)}, u32[]{:S(2)}, u32[]{:S(2)}) %collective-permute-start.8) | collective-permute-done | bytes 81952 | tf_op jit(solution)/shard_map/ppermute | solution.py:259
  66.6 0.7 pad_maximum_fusion.1
  (20 shorter events, 0.5 us)
Async XLA Ops:
  0.0 14.3 %copy-start.1 = (f32[8]{0:T(128)S(1)}, f32[8]{0:T(128)}, u32[]{:S(2)}) copy-start(f32[8]{0:T(128)} %density_ref.3) | copy-start | bytes 100
  0.0 14.3 %copy-start = (f32[3,8]{1,0:T(4,128)S(1)}, f32[3,8]{1,0:T(4,128)}, u32[]{:S(2)}) copy-start(f32[3,8]{1,0:T(4,128)} %color_ref.3) | copy-start | bytes 292
  4.9 6.2 %collective-permute-start = (f32[10,32,128]{2,1,0:T(8,128)S(1)}, f32[10,32,128]{2,1,0:T(8,128)S(1)}, u32[]{:S(2)}, u32[]{:S(2)}) collective-permute-start(f32[10,32,128]{2,1,0:T(8,128)S(1)} %get-tuple-element.15), channel_id=1, source_target_pairs={{0,1},{2,3},{4,5},{6,7},{1,0},{3,2},{5,4},{7,6},{8,9},{10,11},{12,... | collective-permute-start | bytes 491528 | tf_op jit(solution)/shard_map/ppermute | solution.py:236
  6.9 4.2 %collective-permute-start.1 = (f32[10,32,128]{2,1,0:T(8,128)S(1)}, f32[10,32,128]{2,1,0:T(8,128)S(1)}, u32[]{:S(2)}, u32[]{:S(2)}) collective-permute-start(f32[10,32,128]{2,1,0:T(8,128)S(1)} %get-tuple-element.16), channel_id=1, source_target_pairs={{1,2},{3,4},{5,6},{2,1},{4,3},{6,5},{9,10},{11,12},{13,14},{10,9},... | collective-permute-start | bytes 491528 | tf_op jit(solution)/shard_map/ppermute | solution.py:237
  7.5 3.5 %collective-permute-start.2 = (f32[10,32,128]{2,1,0:T(8,128)S(1)}, f32[10,32,128]{2,1,0:T(8,128)S(1)}, u32[]{:S(2)}, u32[]{:S(2)}) collective-permute-start(f32[10,32,128]{2,1,0:T(8,128)S(1)} %get-tuple-element.17), channel_id=1, source_target_pairs={{0,8},{16,24},{32,40},{48,56},{64,72},{80,88},{96,104},{112,120},{... | collective-permute-start | bytes 491528 | tf_op jit(solution)/shard_map/ppermute | solution.py:238
  7.6 6.6 %collective-permute-start.3 = (f32[10,32,128]{2,1,0:T(8,128)S(1)}, f32[10,32,128]{2,1,0:T(8,128)S(1)}, u32[]{:S(2)}, u32[]{:S(2)}) collective-permute-start(f32[10,32,128]{2,1,0:T(8,128)S(1)} %get-tuple-element.17), channel_id=1, source_target_pairs={{8,16},{24,32},{40,48},{56,64},{72,80},{88,96},{104,112},{120,128}... | collective-permute-start | bytes 491528 | tf_op jit(solution)/shard_map/ppermute | solution.py:239
  31.8 13.6 %collective-permute-start.4 = (f32[4,7,4,4,128]{4,3,2,1,0:T(4,128)S(1)}, f32[4,7,4,4,128]{4,3,2,1,0:T(4,128)S(1)}, u32[]{:S(2)}, u32[]{:S(2)}) collective-permute-start(f32[4,7,4,4,128]{4,3,2,1,0:T(4,128)S(1)} %get-tuple-element.20), channel_id=1, source_target_pairs={{0,1},{1,0},{2,3},{3,2},{4,5},{5,4},{6,7},{7,6},{8,9},{9,8},{10,11... | collective-permute-start | bytes 688136 | tf_op jit(solution)/shard_map/ppermute | solution.py:259
  45.4 4.7 %collective-permute-start.6 = (f32[4,3,4,4,128]{4,3,2,1,0:T(4,128)S(1)}, f32[4,3,4,4,128]{4,3,2,1,0:T(4,128)S(1)}, u32[]{:S(2)}, u32[]{:S(2)}) collective-permute-start(f32[4,3,4,4,128]{4,3,2,1,0:T(4,128)S(1)} %get-tuple-element.24), channel_id=1, source_target_pairs={{0,1},{1,0},{2,3},{3,2},{4,5},{5,4},{6,7},{7,6},{8,9},{9,8},{10,11... | collective-permute-start | bytes 294920 | tf_op jit(solution)/shard_map/ppermute | solution.py:259
  45.7 8.2 %collective-permute-start.5 = (f32[2,7,4,4,128]{4,3,2,1,0:T(4,128)S(1)}, f32[2,7,4,4,128]{4,3,2,1,0:T(4,128)S(1)}, u32[]{:S(2)}, u32[]{:S(2)}) collective-permute-start(f32[2,7,4,4,128]{4,3,2,1,0:T(4,128)S(1)} %broadcast_select_fusion.2), channel_id=1, source_target_pairs={{0,2},{1,3},{2,0},{3,1},{4,6},{5,7},{6,4},{7,5},{8,10},{9,11},{10,... | collective-permute-start | bytes 344072 | tf_op jit(solution)/shard_map/ppermute | solution.py:259
  50.2 8.5 %collective-permute-start.7 = (f32[2,3,4,4,128]{4,3,2,1,0:T(4,128)S(1)}, f32[2,3,4,4,128]{4,3,2,1,0:T(4,128)S(1)}, u32[]{:S(2)}, u32[]{:S(2)}) collective-permute-start(f32[2,3,4,4,128]{4,3,2,1,0:T(4,128)S(1)} %broadcast_select_fusion.10), channel_id=1, source_target_pairs={{0,2},{1,3},{2,0},{3,1},{4,6},{5,7},{6,4},{7,5},{8,10},{9,11},{10,... | collective-permute-start | bytes 147464 | tf_op jit(solution)/shard_map/ppermute | solution.py:259
  58.9 7.5 %collective-permute-start.8 = (f32[1,10,4,4,128]{4,3,2,1,0:T(4,128)S(1)}, f32[1,10,4,4,128]{4,3,2,1,0:T(4,128)S(1)}, u32[]{:S(2)}, u32[]{:S(2)}) collective-permute-start(f32[1,10,4,4,128]{4,3,2,1,0:T(4,128)S(1)} %slice_select_fusion), channel_id=1, source_target_pairs={{0,7},{1,6},{2,5},{3,4},{4,3},{5,2},{6,1},{7,0},{8,15},{9,14},{10,... | collective-permute-start | bytes 245768 | tf_op jit(solution)/shard_map/ppermute | solution.py:259

commit v3 on v2

--- a/solution.py
+++ b/solution.py
@@ -9,13 +9,13 @@
 from jax.sharding import PartitionSpec as P
 
 BUMPS = 8
-BASE = 3
 SPACING = 4.0 / (BUMPS - 1)
-CENTRE = -2.0 + SPACING * BASE
 LOG2E = math.log2(math.e)
+LIFT = 49.0
 RATE = 4.0 * SPACING * LOG2E
 BELL = -2.0 * LOG2E / (RATE * RATE)
-FALL = [math.exp(-2.0 * ((j - BASE) * SPACING) ** 2) for j in range(BUMPS)]
+LEAN = -8.0 * LOG2E / RATE
+FALL = [math.exp(-2.0 * (-2.0 + SPACING * j) ** 2) * 2.0**-LIFT for j in range(BUMPS)]
 LANES = 128
 TILE = 8
 PITCH = 40
@@ -122,24 +122,19 @@
             gy = jnp.where(edge_lane, pltpu.roll(rim, LANES - 1 - 2 * z, 1), gy)
             slope = jnp.abs(gz + 0.8 * gx + (16.0 / 15.0) * gy)
             lit = (0.3 / 0.42) + slope * lax.rsqrt(gz * gz + gx * gx + gy * gy + 4.0)
-            q = cell * RATE - (CENTRE * RATE)
-            up = jnp.exp2(q)
-            down = jnp.exp2(-q)
-            bell = jnp.exp2(q * q * BELL)
-            high = (((dens[7] * up + dens[6]) * up + dens[5]) * up + dens[4]) * up + dens[3]
-            low = ((dens[0] * down + dens[1]) * down + dens[2]) * down
-            total = total + (high + low) * bell
+            u = cell * RATE
+            up = jnp.exp2(u)
+            bell = jnp.exp2((u * BELL + LEAN) * u + LIFT)
+            series = dens[BUMPS - 1]
+            for j in range(BUMPS - 2, -1, -1):
+                series = series * up + dens[j]
+            total = total + series * bell
             behind = jnp.exp2(total)
             power = (clear - behind) * lit * bell
-            sums[BASE] = sums[BASE] + power
-            rise = power
-            for j in range(BASE + 1, BUMPS):
-                rise = rise * up
-                sums[j] = sums[j] + rise
-            drop = power
-            for j in range(BASE - 1, -1, -1):
-                drop = drop * down
-                sums[j] = sums[j] + drop
+            sums[0] = sums[0] + power
+            for j in range(1, BUMPS):
+                power = power * up
+                sums[j] = sums[j] + power
             return (total, behind, cell, after, *sums)
 
         zero = jnp.zeros((TILE, LANES), jnp.float32)

time: 67.4 us -> 66.9 us (level)
  transfers between devices with their start and end apart: 9 -> 9, of which waited for: 5 -> 5; matrix products, arithmetic and copies ran while one was open for 1% -> 1% of each run, Pallas kernels for 13% -> 12%
where the time goes in v3:
time: 66.9 us; the launch traced here: 66.8 us
  Pallas kernels  30.3 us (45%)
  starting transfers between devices  18.9 us (28%)
  waiting for transfers between devices  16 us (24%)
  other arithmetic  1.26 us (2%)
    pallas_call x2, Pallas kernels, render(): pl.pallas_call(functools.partial(render_kernel, step=step, start=start),...  25.5 us
    ppermute x5, starting transfers between devices, swapped(): return lax.ppermute(value, 'gz', [(i, partner(i)) for i in range(nz)])  13.4 us
    ppermute x5, waiting for transfers between devices, swapped(): return lax.ppermute(value, 'gz', [(i, partner(i)) for i in range(nz)])  12.1 us
    pallas_call x1, Pallas kernels, local(): pl.pallas_call(edges_kernel, in_specs=[anywhere], out_specs=[vmem] * 4, o...  4.85 us
    ppermute x1, waiting for transfers between devices, local(): y2 = lax.ppermute(outer, 'gy', pairs_of(ny, 1))  3.2 us
    ppermute x1, starting transfers between devices, local(): y2 = lax.ppermute(outer, 'gy', pairs_of(ny, 1))  2.74 us
    ppermute x1, starting transfers between devices, local(): z1 = lax.ppermute(pair, 'gz', pairs_of(nz, 0))  2 us
  transfers between devices with their start and end apart: 9, of which 5 were waited for; matrix products, arithmetic and copies ran while one was open for 1% of the time, Pallas kernels for 12%

profile of v3, /device:TPU:28, one launch (start us, length us, event | category | flops | bytes accessed | tf_op | source)
XLA Modules:
  0.0 66.8 jit_solution(12925199795946075839)
XLA Ops:
  0.0 0.0 copy-start.1
  0.0 0.0 copy-start
  0.0 4.8 %edges.1 = (f32[10,32,128]{2,1,0:T(8,128)S(1)}, f32[10,32,128]{2,1,0:T(8,128)S(1)}, f32[10,32,128]{2,1,0:T(8,128)S(1)}, f32[10,32,128]{2,1,0:T(8,128)S(1)}) custom-call(f32[10,64,32,128]{3,2,1,0:T(8,128)} %field_ref.5), custom_call_target="tpu_custom_call" | custom-call | tf_op jit(solution)/shard_map/edges/pallas_call | solution.py:222
  4.9 2.0 %collective-permute-start = (f32[10,32,128]{2,1,0:T(8,128)S(1)}, f32[10,32,128]{2,1,0:T(8,128)S(1)}, u32[]{:S(2)}, u32[]{:S(2)}) collective-permute-start(f32[10,32,128]{2,1,0:T(8,128)S(1)} %get-tuple-element.15), channel_id=1, source_target_pairs={{0,1},{2,3},{4,5},{6,7},{1,0},{3,2},{5,4},{7,6},{8,9},{10,11},{12,... | collective-permute-start | bytes 491528 | tf_op jit(solution)/shard_map/ppermute | solution.py:231
  6.9 0.7 collective-permute-start.1
  7.5 0.1 collective-permute-start.2
  7.6 2.7 %collective-permute-start.3 = (f32[10,32,128]{2,1,0:T(8,128)S(1)}, f32[10,32,128]{2,1,0:T(8,128)S(1)}, u32[]{:S(2)}, u32[]{:S(2)}) collective-permute-start(f32[10,32,128]{2,1,0:T(8,128)S(1)} %get-tuple-element.17), channel_id=1, source_target_pairs={{8,16},{24,32},{40,48},{56,64},{72,80},{88,96},{104,112},{120,128}... | collective-permute-start | bytes 491528 | tf_op jit(solution)/shard_map/ppermute | solution.py:234
  10.4 0.6 collective-permute-done.z1_ref
  11.1 0.0 collective-permute-done.1.z2_ref
  11.1 0.0 collective-permute-done.2.y1_ref
  11.1 3.2 %collective-permute-done.3.y2_ref = f32[10,32,128]{2,1,0:T(8,128)S(1)} collective-permute-done((f32[10,32,128]{2,1,0:T(8,128)S(1)}, f32[10,32,128]{2,1,0:T(8,128)S(1)}, u32[]{:S(2)}, u32[]{:S(2)}) %collective-permute-start.3) | collective-permute-done | bytes 163872 | tf_op jit(solution)/shard_map/ppermute | solution.py:234
  14.3 0.0 copy-done.1
  14.3 0.0 copy-done
  14.3 17.2 %render_a.1 = (f32[4,7,4,4,128]{4,3,2,1,0:T(4,128)S(1)}, f32[4,7,4,4,128]{4,3,2,1,0:T(4,128)S(1)}) custom-call(f32[8]{0:T(128)S(1)} %copy-done.1, f32[3,8]{1,0:T(4,128)S(1)} %copy-done, f32[10,32,128]{2,1,0:T(8,128)S(1)} %collective-permute-done.z1_ref, f32[10,32,128]{2,1,0:T(8,128)S(1)} %collective-permute-done.1.z2_ref, ...), custom_call_target="tpu_custom_call" | custom-call | flops 22020096000 | bytes 7340032 | tf_op jit(solution)/shard_map/render_a/pallas_call | solution.py:239
  31.5 5.2 %collective-permute-start.4 = (f32[4,7,4,4,128]{4,3,2,1,0:T(4,128)S(1)}, f32[4,7,4,4,128]{4,3,2,1,0:T(4,128)S(1)}, u32[]{:S(2)}, u32[]{:S(2)}) collective-permute-start(f32[4,7,4,4,128]{4,3,2,1,0:T(4,128)S(1)} %get-tuple-element.20), channel_id=1, source_target_pairs={{0,1},{1,0},{2,3},{3,2},{4,5},{5,4},{6,7},{7,6},{8,9},{9,8},{10,11... | collective-permute-start | bytes 688136 | tf_op jit(solution)/shard_map/ppermute | solution.py:254
  36.6 8.3 %render_b.1 = (f32[4,3,4,4,128]{4,3,2,1,0:T(4,128)S(1)}, f32[4,3,4,4,128]{4,3,2,1,0:T(4,128)S(1)}) custom-call(f32[8]{0:T(128)S(1)} %copy-done.1, f32[3,8]{1,0:T(4,128)S(1)} %copy-done, f32[10,32,128]{2,1,0:T(8,128)S(1)} %collective-permute-done.z1_ref, f32[10,32,128]{2,1,0:T(8,128)S(1)} %collective-permute-done.1.z2_ref, ...), custom_call_target="tpu_custom_call" | custom-call | flops 9437184000 | bytes 3145728 | tf_op jit(solution)/shard_map/render_b/pallas_call | solution.py:239
  44.9 0.0 collective-permute-done.4
  44.9 0.1 collective-permute-start.6
  45.1 0.1 fusion
  45.2 3.7 %collective-permute-start.5 = (f32[2,7,4,4,128]{4,3,2,1,0:T(4,128)S(1)}, f32[2,7,4,4,128]{4,3,2,1,0:T(4,128)S(1)}, u32[]{:S(2)}, u32[]{:S(2)}) collective-permute-start(f32[2,7,4,4,128]{4,3,2,1,0:T(4,128)S(1)} %broadcast_select_fusion.2), channel_id=1, source_target_pairs={{0,2},{1,3},{2,0},{3,1},{4,6},{5,7},{6,4},{7,5},{8,10},{9,11},{10,... | collective-permute-start | bytes 344072 | tf_op jit(solution)/shard_map/ppermute | solution.py:254
  48.9 0.7 %collective-permute-done.6 = f32[4,3,4,4,128]{4,3,2,1,0:T(4,128)S(1)} collective-permute-done((f32[4,3,4,4,128]{4,3,2,1,0:T(4,128)S(1)}, f32[4,3,4,4,128]{4,3,2,1,0:T(4,128)S(1)}, u32[]{:S(2)}, u32[]{:S(2)}) %collective-permute-start.6) | collective-permute-done | bytes 98336 | tf_op jit(solution)/shard_map/ppermute | solution.py:254
  49.8 3.7 %collective-permute-start.7 = (f32[2,3,4,4,128]{4,3,2,1,0:T(4,128)S(1)}, f32[2,3,4,4,128]{4,3,2,1,0:T(4,128)S(1)}, u32[]{:S(2)}, u32[]{:S(2)}) collective-permute-start(f32[2,3,4,4,128]{4,3,2,1,0:T(4,128)S(1)} %broadcast_select_fusion.10), channel_id=1, source_target_pairs={{0,2},{1,3},{2,0},{3,1},{4,6},{5,7},{6,4},{7,5},{8,10},{9,11},{10,... | collective-permute-start | bytes 147464 | tf_op jit(solution)/shard_map/ppermute | solution.py:254
  53.4 0.0 collective-permute-done.5
  53.4 0.1 broadcast_select_fusion.5
  53.6 4.7 %collective-permute-done.7 = f32[2,3,4,4,128]{4,3,2,1,0:T(4,128)S(1)} collective-permute-done((f32[2,3,4,4,128]{4,3,2,1,0:T(4,128)S(1)}, f32[2,3,4,4,128]{4,3,2,1,0:T(4,128)S(1)}, u32[]{:S(2)}, u32[]{:S(2)}) %collective-permute-start.7) | collective-permute-done | bytes 49184 | tf_op jit(solution)/shard_map/ppermute | solution.py:254
  58.4 0.8 %collective-permute-start.8 = (f32[1,10,4,4,128]{4,3,2,1,0:T(4,128)S(1)}, f32[1,10,4,4,128]{4,3,2,1,0:T(4,128)S(1)}, u32[]{:S(2)}, u32[]{:S(2)}) collective-permute-start(f32[1,10,4,4,128]{4,3,2,1,0:T(4,128)S(1)} %slice_select_fusion), channel_id=1, source_target_pairs={{0,7},{1,6},{2,5},{3,4},{4,3},{5,2},{6,1},{7,0},{8,15},{9,14},{10,... | collective-permute-start | bytes 245768 | tf_op jit(solution)/shard_map/ppermute | solution.py:254
  59.3 6.7 %collective-permute-done.8 = f32[1,10,4,4,128]{4,3,2,1,0:T(4,128)S(1)} collective-permute-done((f32[1,10,4,4,128]{4,3,2,1,0:T(4,128)S(1)}, f32[1,10,4,4,128]{4,3,2,1,0:T(4,128)S(1)}, u32[]{:S(2)}, u32[]{:S(2)}) %collective-permute-start.8) | collective-permute-done | bytes 81952 | tf_op jit(solution)/shard_map/ppermute | solution.py:254
  66.1 0.7 pad_maximum_fusion.1
  (20 shorter events, 0.5 us)
Async XLA Ops:
  0.0 14.3 %copy-start.1 = (f32[8]{0:T(128)S(1)}, f32[8]{0:T(128)}, u32[]{:S(2)}) copy-start(f32[8]{0:T(128)} %density_ref.3) | copy-start | bytes 100
  0.0 14.3 %copy-start = (f32[3,8]{1,0:T(4,128)S(1)}, f32[3,8]{1,0:T(4,128)}, u32[]{:S(2)}) copy-start(f32[3,8]{1,0:T(4,128)} %color_ref.3) | copy-start | bytes 292
  4.9 6.2 %collective-permute-start = (f32[10,32,128]{2,1,0:T(8,128)S(1)}, f32[10,32,128]{2,1,0:T(8,128)S(1)}, u32[]{:S(2)}, u32[]{:S(2)}) collective-permute-start(f32[10,32,128]{2,1,0:T(8,128)S(1)} %get-tuple-element.15), channel_id=1, source_target_pairs={{0,1},{2,3},{4,5},{6,7},{1,0},{3,2},{5,4},{7,6},{8,9},{10,11},{12,... | collective-permute-start | bytes 491528 | tf_op jit(solution)/shard_map/ppermute | solution.py:231
  6.9 4.2 %collective-permute-start.1 = (f32[10,32,128]{2,1,0:T(8,128)S(1)}, f32[10,32,128]{2,1,0:T(8,128)S(1)}, u32[]{:S(2)}, u32[]{:S(2)}) collective-permute-start(f32[10,32,128]{2,1,0:T(8,128)S(1)} %get-tuple-element.16), channel_id=1, source_target_pairs={{1,2},{3,4},{5,6},{2,1},{4,3},{6,5},{9,10},{11,12},{13,14},{10,9},... | collective-permute-start | bytes 491528 | tf_op jit(solution)/shard_map/ppermute | solution.py:232
  7.5 3.5 %collective-permute-start.2 = (f32[10,32,128]{2,1,0:T(8,128)S(1)}, f32[10,32,128]{2,1,0:T(8,128)S(1)}, u32[]{:S(2)}, u32[]{:S(2)}) collective-permute-start(f32[10,32,128]{2,1,0:T(8,128)S(1)} %get-tuple-element.17), channel_id=1, source_target_pairs={{0,8},{16,24},{32,40},{48,56},{64,72},{80,88},{96,104},{112,120},{... | collective-permute-start | bytes 491528 | tf_op jit(solution)/shard_map/ppermute | solution.py:233
  7.6 6.6 %collective-permute-start.3 = (f32[10,32,128]{2,1,0:T(8,128)S(1)}, f32[10,32,128]{2,1,0:T(8,128)S(1)}, u32[]{:S(2)}, u32[]{:S(2)}) collective-permute-start(f32[10,32,128]{2,1,0:T(8,128)S(1)} %get-tuple-element.17), channel_id=1, source_target_pairs={{8,16},{24,32},{40,48},{56,64},{72,80},{88,96},{104,112},{120,128}... | collective-permute-start | bytes 491528 | tf_op jit(solution)/shard_map/ppermute | solution.py:234
  31.5 13.5 %collective-permute-start.4 = (f32[4,7,4,4,128]{4,3,2,1,0:T(4,128)S(1)}, f32[4,7,4,4,128]{4,3,2,1,0:T(4,128)S(1)}, u32[]{:S(2)}, u32[]{:S(2)}) collective-permute-start(f32[4,7,4,4,128]{4,3,2,1,0:T(4,128)S(1)} %get-tuple-element.20), channel_id=1, source_target_pairs={{0,1},{1,0},{2,3},{3,2},{4,5},{5,4},{6,7},{7,6},{8,9},{9,8},{10,11... | collective-permute-start | bytes 688136 | tf_op jit(solution)/shard_map/ppermute | solution.py:254
  44.9 4.7 %collective-permute-start.6 = (f32[4,3,4,4,128]{4,3,2,1,0:T(4,128)S(1)}, f32[4,3,4,4,128]{4,3,2,1,0:T(4,128)S(1)}, u32[]{:S(2)}, u32[]{:S(2)}) collective-permute-start(f32[4,3,4,4,128]{4,3,2,1,0:T(4,128)S(1)} %get-tuple-element.24), channel_id=1, source_target_pairs={{0,1},{1,0},{2,3},{3,2},{4,5},{5,4},{6,7},{7,6},{8,9},{9,8},{10,11... | collective-permute-start | bytes 294920 | tf_op jit(solution)/shard_map/ppermute | solution.py:254
  45.2 8.2 %collective-permute-start.5 = (f32[2,7,4,4,128]{4,3,2,1,0:T(4,128)S(1)}, f32[2,7,4,4,128]{4,3,2,1,0:T(4,128)S(1)}, u32[]{:S(2)}, u32[]{:S(2)}) collective-permute-start(f32[2,7,4,4,128]{4,3,2,1,0:T(4,128)S(1)} %broadcast_select_fusion.2), channel_id=1, source_target_pairs={{0,2},{1,3},{2,0},{3,1},{4,6},{5,7},{6,4},{7,5},{8,10},{9,11},{10,... | collective-permute-start | bytes 344072 | tf_op jit(solution)/shard_map/ppermute | solution.py:254
  49.8 8.5 %collective-permute-start.7 = (f32[2,3,4,4,128]{4,3,2,1,0:T(4,128)S(1)}, f32[2,3,4,4,128]{4,3,2,1,0:T(4,128)S(1)}, u32[]{:S(2)}, u32[]{:S(2)}) collective-permute-start(f32[2,3,4,4,128]{4,3,2,1,0:T(4,128)S(1)} %broadcast_select_fusion.10), channel_id=1, source_target_pairs={{0,2},{1,3},{2,0},{3,1},{4,6},{5,7},{6,4},{7,5},{8,10},{9,11},{10,... | collective-permute-start | bytes 147464 | tf_op jit(solution)/shard_map/ppermute | solution.py:254
  58.4 7.5 %collective-permute-start.8 = (f32[1,10,4,4,128]{4,3,2,1,0:T(4,128)S(1)}, f32[1,10,4,4,128]{4,3,2,1,0:T(4,128)S(1)}, u32[]{:S(2)}, u32[]{:S(2)}) collective-permute-start(f32[1,10,4,4,128]{4,3,2,1,0:T(4,128)S(1)} %slice_select_fusion), channel_id=1, source_target_pairs={{0,7},{1,6},{2,5},{3,4},{4,3},{5,2},{6,1},{7,0},{8,15},{9,14},{10,... | collective-permute-start | bytes 245768 | tf_op jit(solution)/shard_map/ppermute | solution.py:254

commit v4 on v3

--- a/solution.py
+++ b/solution.py
@@ -185,7 +185,7 @@
             one_tile(frame, slot, t)
             return 0
 
-        lax.fori_loop(0, tiles, with_next, 0)
+        lax.fori_loop(0, tiles, with_next, 0, unroll=4)
         return 0
 
     lax.fori_loop(0, frames, one_frame, 0)

time: 66.9 us -> 66.4 us (level)
  no operation moved by 1% of the time
where the time goes in v4:
time: 66.4 us; the launch traced here: 66.3 us
  Pallas kernels  29.8 us (45%)
  starting transfers between devices  18.9 us (28%)
  waiting for transfers between devices  16 us (24%)
  other arithmetic  1.26 us (2%)
    pallas_call x2, Pallas kernels, render(): pl.pallas_call(functools.partial(render_kernel, step=step, start=start),...  25 us
    ppermute x5, starting transfers between devices, swapped(): return lax.ppermute(value, 'gz', [(i, partner(i)) for i in range(nz)])  13.4 us
    ppermute x5, waiting for transfers between devices, swapped(): return lax.ppermute(value, 'gz', [(i, partner(i)) for i in range(nz)])  12.1 us
    pallas_call x1, Pallas kernels, local(): pl.pallas_call(edges_kernel, in_specs=[anywhere], out_specs=[vmem] * 4, o...  4.85 us
    ppermute x1, waiting for transfers between devices, local(): y2 = lax.ppermute(outer, 'gy', pairs_of(ny, 1))  3.2 us
    ppermute x1, starting transfers between devices, local(): y2 = lax.ppermute(outer, 'gy', pairs_of(ny, 1))  2.74 us
    ppermute x1, starting transfers between devices, local(): z1 = lax.ppermute(pair, 'gz', pairs_of(nz, 0))  2 us
  transfers between devices with their start and end apart: 9, of which 5 were waited for; matrix products, arithmetic and copies ran while one was open for 1% of the time, Pallas kernels for 12%

profile of v4, /device:TPU:28, one launch (start us, length us, event | category | flops | bytes accessed | tf_op | source)
XLA Modules:
  0.0 66.3 jit_solution(4864996088218336533)
XLA Ops:
  0.0 0.0 copy-start.1
  0.0 0.0 copy-start
  0.0 4.8 %edges.1 = (f32[10,32,128]{2,1,0:T(8,128)S(1)}, f32[10,32,128]{2,1,0:T(8,128)S(1)}, f32[10,32,128]{2,1,0:T(8,128)S(1)}, f32[10,32,128]{2,1,0:T(8,128)S(1)}) custom-call(f32[10,64,32,128]{3,2,1,0:T(8,128)} %field_ref.5), custom_call_target="tpu_custom_call" | custom-call | tf_op jit(solution)/shard_map/edges/pallas_call | solution.py:222
  4.9 2.0 %collective-permute-start = (f32[10,32,128]{2,1,0:T(8,128)S(1)}, f32[10,32,128]{2,1,0:T(8,128)S(1)}, u32[]{:S(2)}, u32[]{:S(2)}) collective-permute-start(f32[10,32,128]{2,1,0:T(8,128)S(1)} %get-tuple-element.15), channel_id=1, source_target_pairs={{0,1},{2,3},{4,5},{6,7},{1,0},{3,2},{5,4},{7,6},{8,9},{10,11},{12,... | collective-permute-start | bytes 491528 | tf_op jit(solution)/shard_map/ppermute | solution.py:231
  6.9 0.7 collective-permute-start.1
  7.5 0.1 collective-permute-start.2
  7.6 2.7 %collective-permute-start.3 = (f32[10,32,128]{2,1,0:T(8,128)S(1)}, f32[10,32,128]{2,1,0:T(8,128)S(1)}, u32[]{:S(2)}, u32[]{:S(2)}) collective-permute-start(f32[10,32,128]{2,1,0:T(8,128)S(1)} %get-tuple-element.17), channel_id=1, source_target_pairs={{8,16},{24,32},{40,48},{56,64},{72,80},{88,96},{104,112},{120,128}... | collective-permute-start | bytes 491528 | tf_op jit(solution)/shard_map/ppermute | solution.py:234
  10.4 0.6 collective-permute-done.z1_ref
  11.1 0.0 collective-permute-done.1.z2_ref
  11.1 0.0 collective-permute-done.2.y1_ref
  11.1 3.2 %collective-permute-done.3.y2_ref = f32[10,32,128]{2,1,0:T(8,128)S(1)} collective-permute-done((f32[10,32,128]{2,1,0:T(8,128)S(1)}, f32[10,32,128]{2,1,0:T(8,128)S(1)}, u32[]{:S(2)}, u32[]{:S(2)}) %collective-permute-start.3) | collective-permute-done | bytes 163872 | tf_op jit(solution)/shard_map/ppermute | solution.py:234
  14.3 0.0 copy-done.1
  14.3 0.0 copy-done
  14.3 16.8 %render_a.1 = (f32[4,7,4,4,128]{4,3,2,1,0:T(4,128)S(1)}, f32[4,7,4,4,128]{4,3,2,1,0:T(4,128)S(1)}) custom-call(f32[8]{0:T(128)S(1)} %copy-done.1, f32[3,8]{1,0:T(4,128)S(1)} %copy-done, f32[10,32,128]{2,1,0:T(8,128)S(1)} %collective-permute-done.z1_ref, f32[10,32,128]{2,1,0:T(8,128)S(1)} %collective-permute-done.1.z2_ref, ...), custom_call_target="tpu_custom_call" | custom-call | flops 22020096000 | bytes 7340032 | tf_op jit(solution)/shard_map/render_a/pallas_call | solution.py:239
  31.1 5.2 %collective-permute-start.4 = (f32[4,7,4,4,128]{4,3,2,1,0:T(4,128)S(1)}, f32[4,7,4,4,128]{4,3,2,1,0:T(4,128)S(1)}, u32[]{:S(2)}, u32[]{:S(2)}) collective-permute-start(f32[4,7,4,4,128]{4,3,2,1,0:T(4,128)S(1)} %get-tuple-element.20), channel_id=1, source_target_pairs={{0,1},{1,0},{2,3},{3,2},{4,5},{5,4},{6,7},{7,6},{8,9},{9,8},{10,11... | collective-permute-start | bytes 688136 | tf_op jit(solution)/shard_map/ppermute | solution.py:254
  36.3 8.1 %render_b.1 = (f32[4,3,4,4,128]{4,3,2,1,0:T(4,128)S(1)}, f32[4,3,4,4,128]{4,3,2,1,0:T(4,128)S(1)}) custom-call(f32[8]{0:T(128)S(1)} %copy-done.1, f32[3,8]{1,0:T(4,128)S(1)} %copy-done, f32[10,32,128]{2,1,0:T(8,128)S(1)} %collective-permute-done.z1_ref, f32[10,32,128]{2,1,0:T(8,128)S(1)} %collective-permute-done.1.z2_ref, ...), custom_call_target="tpu_custom_call" | custom-call | flops 9437184000 | bytes 3145728 | tf_op jit(solution)/shard_map/render_b/pallas_call | solution.py:239
  44.4 0.0 collective-permute-done.4
  44.4 0.1 collective-permute-start.6
  44.6 0.1 fusion
  44.7 3.7 %collective-permute-start.5 = (f32[2,7,4,4,128]{4,3,2,1,0:T(4,128)S(1)}, f32[2,7,4,4,128]{4,3,2,1,0:T(4,128)S(1)}, u32[]{:S(2)}, u32[]{:S(2)}) collective-permute-start(f32[2,7,4,4,128]{4,3,2,1,0:T(4,128)S(1)} %broadcast_select_fusion.2), channel_id=1, source_target_pairs={{0,2},{1,3},{2,0},{3,1},{4,6},{5,7},{6,4},{7,5},{8,10},{9,11},{10,... | collective-permute-start | bytes 344072 | tf_op jit(solution)/shard_map/ppermute | solution.py:254
  48.4 0.7 %collective-permute-done.6 = f32[4,3,4,4,128]{4,3,2,1,0:T(4,128)S(1)} collective-permute-done((f32[4,3,4,4,128]{4,3,2,1,0:T(4,128)S(1)}, f32[4,3,4,4,128]{4,3,2,1,0:T(4,128)S(1)}, u32[]{:S(2)}, u32[]{:S(2)}) %collective-permute-start.6) | collective-permute-done | bytes 98336 | tf_op jit(solution)/shard_map/ppermute | solution.py:254
  49.2 3.7 %collective-permute-start.7 = (f32[2,3,4,4,128]{4,3,2,1,0:T(4,128)S(1)}, f32[2,3,4,4,128]{4,3,2,1,0:T(4,128)S(1)}, u32[]{:S(2)}, u32[]{:S(2)}) collective-permute-start(f32[2,3,4,4,128]{4,3,2,1,0:T(4,128)S(1)} %broadcast_select_fusion.10), channel_id=1, source_target_pairs={{0,2},{1,3},{2,0},{3,1},{4,6},{5,7},{6,4},{7,5},{8,10},{9,11},{10,... | collective-permute-start | bytes 147464 | tf_op jit(solution)/shard_map/ppermute | solution.py:254
  52.9 0.0 collective-permute-done.5
  52.9 0.1 broadcast_select_fusion.5
  53.1 4.7 %collective-permute-done.7 = f32[2,3,4,4,128]{4,3,2,1,0:T(4,128)S(1)} collective-permute-done((f32[2,3,4,4,128]{4,3,2,1,0:T(4,128)S(1)}, f32[2,3,4,4,128]{4,3,2,1,0:T(4,128)S(1)}, u32[]{:S(2)}, u32[]{:S(2)}) %collective-permute-start.7) | collective-permute-done | bytes 49184 | tf_op jit(solution)/shard_map/ppermute | solution.py:254
  57.9 0.8 %collective-permute-start.8 = (f32[1,10,4,4,128]{4,3,2,1,0:T(4,128)S(1)}, f32[1,10,4,4,128]{4,3,2,1,0:T(4,128)S(1)}, u32[]{:S(2)}, u32[]{:S(2)}) collective-permute-start(f32[1,10,4,4,128]{4,3,2,1,0:T(4,128)S(1)} %slice_select_fusion), channel_id=1, source_target_pairs={{0,7},{1,6},{2,5},{3,4},{4,3},{5,2},{6,1},{7,0},{8,15},{9,14},{10,... | collective-permute-start | bytes 245768 | tf_op jit(solution)/shard_map/ppermute | solution.py:254
  58.8 6.7 %collective-permute-done.8 = f32[1,10,4,4,128]{4,3,2,1,0:T(4,128)S(1)} collective-permute-done((f32[1,10,4,4,128]{4,3,2,1,0:T(4,128)S(1)}, f32[1,10,4,4,128]{4,3,2,1,0:T(4,128)S(1)}, u32[]{:S(2)}, u32[]{:S(2)}) %collective-permute-start.8) | collective-permute-done | bytes 81952 | tf_op jit(solution)/shard_map/ppermute | solution.py:254
  65.6 0.7 pad_maximum_fusion.1
  (20 shorter events, 0.5 us)
Async XLA Ops:
  0.0 14.3 %copy-start.1 = (f32[8]{0:T(128)S(1)}, f32[8]{0:T(128)}, u32[]{:S(2)}) copy-start(f32[8]{0:T(128)} %density_ref.3) | copy-start | bytes 100
  0.0 14.3 %copy-start = (f32[3,8]{1,0:T(4,128)S(1)}, f32[3,8]{1,0:T(4,128)}, u32[]{:S(2)}) copy-start(f32[3,8]{1,0:T(4,128)} %color_ref.3) | copy-start | bytes 292
  4.9 6.2 %collective-permute-start = (f32[10,32,128]{2,1,0:T(8,128)S(1)}, f32[10,32,128]{2,1,0:T(8,128)S(1)}, u32[]{:S(2)}, u32[]{:S(2)}) collective-permute-start(f32[10,32,128]{2,1,0:T(8,128)S(1)} %get-tuple-element.15), channel_id=1, source_target_pairs={{0,1},{2,3},{4,5},{6,7},{1,0},{3,2},{5,4},{7,6},{8,9},{10,11},{12,... | collective-permute-start | bytes 491528 | tf_op jit(solution)/shard_map/ppermute | solution.py:231
  6.9 4.2 %collective-permute-start.1 = (f32[10,32,128]{2,1,0:T(8,128)S(1)}, f32[10,32,128]{2,1,0:T(8,128)S(1)}, u32[]{:S(2)}, u32[]{:S(2)}) collective-permute-start(f32[10,32,128]{2,1,0:T(8,128)S(1)} %get-tuple-element.16), channel_id=1, source_target_pairs={{1,2},{3,4},{5,6},{2,1},{4,3},{6,5},{9,10},{11,12},{13,14},{10,9},... | collective-permute-start | bytes 491528 | tf_op jit(solution)/shard_map/ppermute | solution.py:232
  7.5 3.5 %collective-permute-start.2 = (f32[10,32,128]{2,1,0:T(8,128)S(1)}, f32[10,32,128]{2,1,0:T(8,128)S(1)}, u32[]{:S(2)}, u32[]{:S(2)}) collective-permute-start(f32[10,32,128]{2,1,0:T(8,128)S(1)} %get-tuple-element.17), channel_id=1, source_target_pairs={{0,8},{16,24},{32,40},{48,56},{64,72},{80,88},{96,104},{112,120},{... | collective-permute-start | bytes 491528 | tf_op jit(solution)/shard_map/ppermute | solution.py:233
  7.6 6.6 %collective-permute-start.3 = (f32[10,32,128]{2,1,0:T(8,128)S(1)}, f32[10,32,128]{2,1,0:T(8,128)S(1)}, u32[]{:S(2)}, u32[]{:S(2)}) collective-permute-start(f32[10,32,128]{2,1,0:T(8,128)S(1)} %get-tuple-element.17), channel_id=1, source_target_pairs={{8,16},{24,32},{40,48},{56,64},{72,80},{88,96},{104,112},{120,128}... | collective-permute-start | bytes 491528 | tf_op jit(solution)/shard_map/ppermute | solution.py:234
  31.1 13.3 %collective-permute-start.4 = (f32[4,7,4,4,128]{4,3,2,1,0:T(4,128)S(1)}, f32[4,7,4,4,128]{4,3,2,1,0:T(4,128)S(1)}, u32[]{:S(2)}, u32[]{:S(2)}) collective-permute-start(f32[4,7,4,4,128]{4,3,2,1,0:T(4,128)S(1)} %get-tuple-element.20), channel_id=1, source_target_pairs={{0,1},{1,0},{2,3},{3,2},{4,5},{5,4},{6,7},{7,6},{8,9},{9,8},{10,11... | collective-permute-start | bytes 688136 | tf_op jit(solution)/shard_map/ppermute | solution.py:254
  44.4 4.7 %collective-permute-start.6 = (f32[4,3,4,4,128]{4,3,2,1,0:T(4,128)S(1)}, f32[4,3,4,4,128]{4,3,2,1,0:T(4,128)S(1)}, u32[]{:S(2)}, u32[]{:S(2)}) collective-permute-start(f32[4,3,4,4,128]{4,3,2,1,0:T(4,128)S(1)} %get-tuple-element.24), channel_id=1, source_target_pairs={{0,1},{1,0},{2,3},{3,2},{4,5},{5,4},{6,7},{7,6},{8,9},{9,8},{10,11... | collective-permute-start | bytes 294920 | tf_op jit(solution)/shard_map/ppermute | solution.py:254
  44.7 8.2 %collective-permute-start.5 = (f32[2,7,4,4,128]{4,3,2,1,0:T(4,128)S(1)}, f32[2,7,4,4,128]{4,3,2,1,0:T(4,128)S(1)}, u32[]{:S(2)}, u32[]{:S(2)}) collective-permute-start(f32[2,7,4,4,128]{4,3,2,1,0:T(4,128)S(1)} %broadcast_select_fusion.2), channel_id=1, source_target_pairs={{0,2},{1,3},{2,0},{3,1},{4,6},{5,7},{6,4},{7,5},{8,10},{9,11},{10,... | collective-permute-start | bytes 344072 | tf_op jit(solution)/shard_map/ppermute | solution.py:254
  49.2 8.5 %collective-permute-start.7 = (f32[2,3,4,4,128]{4,3,2,1,0:T(4,128)S(1)}, f32[2,3,4,4,128]{4,3,2,1,0:T(4,128)S(1)}, u32[]{:S(2)}, u32[]{:S(2)}) collective-permute-start(f32[2,3,4,4,128]{4,3,2,1,0:T(4,128)S(1)} %broadcast_select_fusion.10), channel_id=1, source_target_pairs={{0,2},{1,3},{2,0},{3,1},{4,6},{5,7},{6,4},{7,5},{8,10},{9,11},{10,... | collective-permute-start | bytes 147464 | tf_op jit(solution)/shard_map/ppermute | solution.py:254
  57.9 7.5 %collective-permute-start.8 = (f32[1,10,4,4,128]{4,3,2,1,0:T(4,128)S(1)}, f32[1,10,4,4,128]{4,3,2,1,0:T(4,128)S(1)}, u32[]{:S(2)}, u32[]{:S(2)}) collective-permute-start(f32[1,10,4,4,128]{4,3,2,1,0:T(4,128)S(1)} %slice_select_fusion), channel_id=1, source_target_pairs={{0,7},{1,6},{2,5},{3,4},{4,3},{5,2},{6,1},{7,0},{8,15},{9,14},{10,... | collective-permute-start | bytes 245768 | tf_op jit(solution)/shard_map/ppermute | solution.py:254

commit v5 on v4

--- a/solution.py
+++ b/solution.py
@@ -165,17 +165,17 @@
     def one_frame(frame, _):
         slot = lax.rem(frame, 2)
 
-        @pl.when(frame + 1 < frames)
-        def _():
-            for t in range(tiles):
-                load(frame + 1, 1 - slot, t).start()
-
         for t in range(tiles):
             here, there = slice(t * TILE, (t + 1) * TILE), slice((t + 1) * TILE, (t + 2) * TILE)
             a, b = z1_ref[start + frame, here, :], z2_ref[start + frame, here, :]
             cells[slot, 0, there, :] = jnp.where(odd_z, a, b)
             cells[slot, depth + 1, there, :] = jnp.where(odd_z, b, a)
         load(frame, slot, 0).wait()
+
+        @pl.when(frame + 1 < frames)
+        def _():
+            for t in range(tiles):
+                load(frame + 1, 1 - slot, t).start()
 
         def with_next(t, _):
             @pl.when(t + 1 < tiles)

time: 66.4 us -> 66.4 us (level)
  no operation moved by 1% of the time
where the time goes in v5:
time: 66.4 us; the launch traced here: 66.3 us
  Pallas kernels  29.8 us (45%)
  starting transfers between devices  18.9 us (28%)
  waiting for transfers between devices  16 us (24%)
  other arithmetic  1.26 us (2%)
    pallas_call x2, Pallas kernels, render(): pl.pallas_call(functools.partial(render_kernel, step=step, start=start),...  25 us
    ppermute x5, starting transfers between devices, swapped(): return lax.ppermute(value, 'gz', [(i, partner(i)) for i in range(nz)])  13.4 us
    ppermute x5, waiting for transfers between devices, swapped(): return lax.ppermute(value, 'gz', [(i, partner(i)) for i in range(nz)])  12.1 us
    pallas_call x1, Pallas kernels, local(): pl.pallas_call(edges_kernel, in_specs=[anywhere], out_specs=[vmem] * 4, o...  4.85 us
    ppermute x1, waiting for transfers between devices, local(): y2 = lax.ppermute(outer, 'gy', pairs_of(ny, 1))  3.2 us
    ppermute x1, starting transfers between devices, local(): y2 = lax.ppermute(outer, 'gy', pairs_of(ny, 1))  2.74 us
    ppermute x1, starting transfers between devices, local(): z1 = lax.ppermute(pair, 'gz', pairs_of(nz, 0))  2 us
  transfers between devices with their start and end apart: 9, of which 5 were waited for; matrix products, arithmetic and copies ran while one was open for 1% of the time, Pallas kernels for 12%

profile of v5, /device:TPU:28, one launch (start us, length us, event | category | flops | bytes accessed | tf_op | source)
XLA Modules:
  0.0 66.3 jit_solution(7283274831401513694)
XLA Ops:
  0.0 0.0 copy-start.1
  0.0 0.0 copy-start
  0.0 4.8 %edges.1 = (f32[10,32,128]{2,1,0:T(8,128)S(1)}, f32[10,32,128]{2,1,0:T(8,128)S(1)}, f32[10,32,128]{2,1,0:T(8,128)S(1)}, f32[10,32,128]{2,1,0:T(8,128)S(1)}) custom-call(f32[10,64,32,128]{3,2,1,0:T(8,128)} %field_ref.5), custom_call_target="tpu_custom_call" | custom-call | tf_op jit(solution)/shard_map/edges/pallas_call | solution.py:222
  4.9 2.0 %collective-permute-start = (f32[10,32,128]{2,1,0:T(8,128)S(1)}, f32[10,32,128]{2,1,0:T(8,128)S(1)}, u32[]{:S(2)}, u32[]{:S(2)}) collective-permute-start(f32[10,32,128]{2,1,0:T(8,128)S(1)} %get-tuple-element.15), channel_id=1, source_target_pairs={{0,1},{2,3},{4,5},{6,7},{1,0},{3,2},{5,4},{7,6},{8,9},{10,11},{12,... | collective-permute-start | bytes 491528 | tf_op jit(solution)/shard_map/ppermute | solution.py:231
  6.9 0.7 collective-permute-start.1
  7.5 0.1 collective-permute-start.2
  7.6 2.7 %collective-permute-start.3 = (f32[10,32,128]{2,1,0:T(8,128)S(1)}, f32[10,32,128]{2,1,0:T(8,128)S(1)}, u32[]{:S(2)}, u32[]{:S(2)}) collective-permute-start(f32[10,32,128]{2,1,0:T(8,128)S(1)} %get-tuple-element.17), channel_id=1, source_target_pairs={{8,16},{24,32},{40,48},{56,64},{72,80},{88,96},{104,112},{120,128}... | collective-permute-start | bytes 491528 | tf_op jit(solution)/shard_map/ppermute | solution.py:234
  10.4 0.6 collective-permute-done.z1_ref
  11.1 0.0 collective-permute-done.1.z2_ref
  11.1 0.0 collective-permute-done.2.y1_ref
  11.1 3.2 %collective-permute-done.3.y2_ref = f32[10,32,128]{2,1,0:T(8,128)S(1)} collective-permute-done((f32[10,32,128]{2,1,0:T(8,128)S(1)}, f32[10,32,128]{2,1,0:T(8,128)S(1)}, u32[]{:S(2)}, u32[]{:S(2)}) %collective-permute-start.3) | collective-permute-done | bytes 163872 | tf_op jit(solution)/shard_map/ppermute | solution.py:234
  14.3 0.0 copy-done.1
  14.3 0.0 copy-done
  14.3 16.8 %render_a.1 = (f32[4,7,4,4,128]{4,3,2,1,0:T(4,128)S(1)}, f32[4,7,4,4,128]{4,3,2,1,0:T(4,128)S(1)}) custom-call(f32[8]{0:T(128)S(1)} %copy-done.1, f32[3,8]{1,0:T(4,128)S(1)} %copy-done, f32[10,32,128]{2,1,0:T(8,128)S(1)} %collective-permute-done.z1_ref, f32[10,32,128]{2,1,0:T(8,128)S(1)} %collective-permute-done.1.z2_ref, ...), custom_call_target="tpu_custom_call" | custom-call | flops 22020096000 | bytes 7340032 | tf_op jit(solution)/shard_map/render_a/pallas_call | solution.py:239
  31.1 5.2 %collective-permute-start.4 = (f32[4,7,4,4,128]{4,3,2,1,0:T(4,128)S(1)}, f32[4,7,4,4,128]{4,3,2,1,0:T(4,128)S(1)}, u32[]{:S(2)}, u32[]{:S(2)}) collective-permute-start(f32[4,7,4,4,128]{4,3,2,1,0:T(4,128)S(1)} %get-tuple-element.20), channel_id=1, source_target_pairs={{0,1},{1,0},{2,3},{3,2},{4,5},{5,4},{6,7},{7,6},{8,9},{9,8},{10,11... | collective-permute-start | bytes 688136 | tf_op jit(solution)/shard_map/ppermute | solution.py:254
  36.3 8.1 %render_b.1 = (f32[4,3,4,4,128]{4,3,2,1,0:T(4,128)S(1)}, f32[4,3,4,4,128]{4,3,2,1,0:T(4,128)S(1)}) custom-call(f32[8]{0:T(128)S(1)} %copy-done.1, f32[3,8]{1,0:T(4,128)S(1)} %copy-done, f32[10,32,128]{2,1,0:T(8,128)S(1)} %collective-permute-done.z1_ref, f32[10,32,128]{2,1,0:T(8,128)S(1)} %collective-permute-done.1.z2_ref, ...), custom_call_target="tpu_custom_call" | custom-call | flops 9437184000 | bytes 3145728 | tf_op jit(solution)/shard_map/render_b/pallas_call | solution.py:239
  44.4 0.0 collective-permute-done.4
  44.4 0.1 collective-permute-start.6
  44.6 0.1 fusion
  44.7 3.7 %collective-permute-start.5 = (f32[2,7,4,4,128]{4,3,2,1,0:T(4,128)S(1)}, f32[2,7,4,4,128]{4,3,2,1,0:T(4,128)S(1)}, u32[]{:S(2)}, u32[]{:S(2)}) collective-permute-start(f32[2,7,4,4,128]{4,3,2,1,0:T(4,128)S(1)} %broadcast_select_fusion.2), channel_id=1, source_target_pairs={{0,2},{1,3},{2,0},{3,1},{4,6},{5,7},{6,4},{7,5},{8,10},{9,11},{10,... | collective-permute-start | bytes 344072 | tf_op jit(solution)/shard_map/ppermute | solution.py:254
  48.4 0.7 %collective-permute-done.6 = f32[4,3,4,4,128]{4,3,2,1,0:T(4,128)S(1)} collective-permute-done((f32[4,3,4,4,128]{4,3,2,1,0:T(4,128)S(1)}, f32[4,3,4,4,128]{4,3,2,1,0:T(4,128)S(1)}, u32[]{:S(2)}, u32[]{:S(2)}) %collective-permute-start.6) | collective-permute-done | bytes 98336 | tf_op jit(solution)/shard_map/ppermute | solution.py:254
  49.2 3.7 %collective-permute-start.7 = (f32[2,3,4,4,128]{4,3,2,1,0:T(4,128)S(1)}, f32[2,3,4,4,128]{4,3,2,1,0:T(4,128)S(1)}, u32[]{:S(2)}, u32[]{:S(2)}) collective-permute-start(f32[2,3,4,4,128]{4,3,2,1,0:T(4,128)S(1)} %broadcast_select_fusion.10), channel_id=1, source_target_pairs={{0,2},{1,3},{2,0},{3,1},{4,6},{5,7},{6,4},{7,5},{8,10},{9,11},{10,... | collective-permute-start | bytes 147464 | tf_op jit(solution)/shard_map/ppermute | solution.py:254
  52.9 0.0 collective-permute-done.5
  52.9 0.1 broadcast_select_fusion.5
  53.0 4.7 %collective-permute-done.7 = f32[2,3,4,4,128]{4,3,2,1,0:T(4,128)S(1)} collective-permute-done((f32[2,3,4,4,128]{4,3,2,1,0:T(4,128)S(1)}, f32[2,3,4,4,128]{4,3,2,1,0:T(4,128)S(1)}, u32[]{:S(2)}, u32[]{:S(2)}) %collective-permute-start.7) | collective-permute-done | bytes 49184 | tf_op jit(solution)/shard_map/ppermute | solution.py:254
  57.9 0.8 %collective-permute-start.8 = (f32[1,10,4,4,128]{4,3,2,1,0:T(4,128)S(1)}, f32[1,10,4,4,128]{4,3,2,1,0:T(4,128)S(1)}, u32[]{:S(2)}, u32[]{:S(2)}) collective-permute-start(f32[1,10,4,4,128]{4,3,2,1,0:T(4,128)S(1)} %slice_select_fusion), channel_id=1, source_target_pairs={{0,7},{1,6},{2,5},{3,4},{4,3},{5,2},{6,1},{7,0},{8,15},{9,14},{10,... | collective-permute-start | bytes 245768 | tf_op jit(solution)/shard_map/ppermute | solution.py:254
  58.7 6.7 %collective-permute-done.8 = f32[1,10,4,4,128]{4,3,2,1,0:T(4,128)S(1)} collective-permute-done((f32[1,10,4,4,128]{4,3,2,1,0:T(4,128)S(1)}, f32[1,10,4,4,128]{4,3,2,1,0:T(4,128)S(1)}, u32[]{:S(2)}, u32[]{:S(2)}) %collective-permute-start.8) | collective-permute-done | bytes 81952 | tf_op jit(solution)/shard_map/ppermute | solution.py:254
  65.6 0.7 pad_maximum_fusion.1
  (20 shorter events, 0.5 us)
Async XLA Ops:
  0.0 14.3 %copy-start.1 = (f32[8]{0:T(128)S(1)}, f32[8]{0:T(128)}, u32[]{:S(2)}) copy-start(f32[8]{0:T(128)} %density_ref.3) | copy-start | bytes 100
  0.0 14.3 %copy-start = (f32[3,8]{1,0:T(4,128)S(1)}, f32[3,8]{1,0:T(4,128)}, u32[]{:S(2)}) copy-start(f32[3,8]{1,0:T(4,128)} %color_ref.3) | copy-start | bytes 292
  4.9 6.2 %collective-permute-start = (f32[10,32,128]{2,1,0:T(8,128)S(1)}, f32[10,32,128]{2,1,0:T(8,128)S(1)}, u32[]{:S(2)}, u32[]{:S(2)}) collective-permute-start(f32[10,32,128]{2,1,0:T(8,128)S(1)} %get-tuple-element.15), channel_id=1, source_target_pairs={{0,1},{2,3},{4,5},{6,7},{1,0},{3,2},{5,4},{7,6},{8,9},{10,11},{12,... | collective-permute-start | bytes 491528 | tf_op jit(solution)/shard_map/ppermute | solution.py:231
  6.9 4.2 %collective-permute-start.1 = (f32[10,32,128]{2,1,0:T(8,128)S(1)}, f32[10,32,128]{2,1,0:T(8,128)S(1)}, u32[]{:S(2)}, u32[]{:S(2)}) collective-permute-start(f32[10,32,128]{2,1,0:T(8,128)S(1)} %get-tuple-element.16), channel_id=1, source_target_pairs={{1,2},{3,4},{5,6},{2,1},{4,3},{6,5},{9,10},{11,12},{13,14},{10,9},... | collective-permute-start | bytes 491528 | tf_op jit(solution)/shard_map/ppermute | solution.py:232
  7.5 3.5 %collective-permute-start.2 = (f32[10,32,128]{2,1,0:T(8,128)S(1)}, f32[10,32,128]{2,1,0:T(8,128)S(1)}, u32[]{:S(2)}, u32[]{:S(2)}) collective-permute-start(f32[10,32,128]{2,1,0:T(8,128)S(1)} %get-tuple-element.17), channel_id=1, source_target_pairs={{0,8},{16,24},{32,40},{48,56},{64,72},{80,88},{96,104},{112,120},{... | collective-permute-start | bytes 491528 | tf_op jit(solution)/shard_map/ppermute | solution.py:233
  7.6 6.6 %collective-permute-start.3 = (f32[10,32,128]{2,1,0:T(8,128)S(1)}, f32[10,32,128]{2,1,0:T(8,128)S(1)}, u32[]{:S(2)}, u32[]{:S(2)}) collective-permute-start(f32[10,32,128]{2,1,0:T(8,128)S(1)} %get-tuple-element.17), channel_id=1, source_target_pairs={{8,16},{24,32},{40,48},{56,64},{72,80},{88,96},{104,112},{120,128}... | collective-permute-start | bytes 491528 | tf_op jit(solution)/shard_map/ppermute | solution.py:234
  31.1 13.3 %collective-permute-start.4 = (f32[4,7,4,4,128]{4,3,2,1,0:T(4,128)S(1)}, f32[4,7,4,4,128]{4,3,2,1,0:T(4,128)S(1)}, u32[]{:S(2)}, u32[]{:S(2)}) collective-permute-start(f32[4,7,4,4,128]{4,3,2,1,0:T(4,128)S(1)} %get-tuple-element.20), channel_id=1, source_target_pairs={{0,1},{1,0},{2,3},{3,2},{4,5},{5,4},{6,7},{7,6},{8,9},{9,8},{10,11... | collective-permute-start | bytes 688136 | tf_op jit(solution)/shard_map/ppermute | solution.py:254
  44.4 4.7 %collective-permute-start.6 = (f32[4,3,4,4,128]{4,3,2,1,0:T(4,128)S(1)}, f32[4,3,4,4,128]{4,3,2,1,0:T(4,128)S(1)}, u32[]{:S(2)}, u32[]{:S(2)}) collective-permute-start(f32[4,3,4,4,128]{4,3,2,1,0:T(4,128)S(1)} %get-tuple-element.24), channel_id=1, source_target_pairs={{0,1},{1,0},{2,3},{3,2},{4,5},{5,4},{6,7},{7,6},{8,9},{9,8},{10,11... | collective-permute-start | bytes 294920 | tf_op jit(solution)/shard_map/ppermute | solution.py:254
  44.7 8.2 %collective-permute-start.5 = (f32[2,7,4,4,128]{4,3,2,1,0:T(4,128)S(1)}, f32[2,7,4,4,128]{4,3,2,1,0:T(4,128)S(1)}, u32[]{:S(2)}, u32[]{:S(2)}) collective-permute-start(f32[2,7,4,4,128]{4,3,2,1,0:T(4,128)S(1)} %broadcast_select_fusion.2), channel_id=1, source_target_pairs={{0,2},{1,3},{2,0},{3,1},{4,6},{5,7},{6,4},{7,5},{8,10},{9,11},{10,... | collective-permute-start | bytes 344072 | tf_op jit(solution)/shard_map/ppermute | solution.py:254
  49.2 8.5 %collective-permute-start.7 = (f32[2,3,4,4,128]{4,3,2,1,0:T(4,128)S(1)}, f32[2,3,4,4,128]{4,3,2,1,0:T(4,128)S(1)}, u32[]{:S(2)}, u32[]{:S(2)}) collective-permute-start(f32[2,3,4,4,128]{4,3,2,1,0:T(4,128)S(1)} %broadcast_select_fusion.10), channel_id=1, source_target_pairs={{0,2},{1,3},{2,0},{3,1},{4,6},{5,7},{6,4},{7,5},{8,10},{9,11},{10,... | collective-permute-start | bytes 147464 | tf_op jit(solution)/shard_map/ppermute | solution.py:254
  57.9 7.5 %collective-permute-start.8 = (f32[1,10,4,4,128]{4,3,2,1,0:T(4,128)S(1)}, f32[1,10,4,4,128]{4,3,2,1,0:T(4,128)S(1)}, u32[]{:S(2)}, u32[]{:S(2)}) collective-permute-start(f32[1,10,4,4,128]{4,3,2,1,0:T(4,128)S(1)} %slice_select_fusion), channel_id=1, source_target_pairs={{0,7},{1,6},{2,5},{3,4},{4,3},{5,2},{6,1},{7,0},{8,15},{9,14},{10,... | collective-permute-start | bytes 245768 | tf_op jit(solution)/shard_map/ppermute | solution.py:254
